TPU v7x, 32 devices: a whole 2x2x4 slice. The times are simulated.
32 devices in a mesh: gx: 4 (over y, x), gy: 8 (over z, core).
Axes of the slice: x: 2, y: 2, z: 4, core: 2. Of those that a mesh axis runs over, the one named last changes fastest.
Arguments:
- noisy_state: bfloat16 [4, 2048, 512], P(None, 'gy', 'gx'), may hold values from -6 to 6
- fresh_noise: bfloat16 [4, 2048, 512], P(None, 'gy', 'gx'), may hold values from -6 to 6
- conditioning: bfloat16 [12, 2048, 512], P(None, 'gy', 'gx'), may hold values from -6 to 6
- first_kernel: bfloat16 [3, 3, 128, 16], replicated, may hold values from -0.5 to 0.5
- first_bias: float32 [128], replicated, may hold values from -4 to 4
- film_weight: bfloat16 [256, 12], replicated, may hold values from -1.75 to 1.75
- film_bias: float32 [256], replicated, may hold values from -3 to 3
- second_kernel: bfloat16 [3, 3, 128, 128], replicated, may hold values from -0.1875 to 0.1875
- second_bias: float32 [128], replicated, may hold values from -4 to 4
- skip_kernel: bfloat16 [128, 16], replicated, may hold values from -1.5 to 1.5
- out_kernel: bfloat16 [4, 128], replicated, may hold values from -0.5 to 0.5
- strip_table: bfloat16 [160, 1024], P('gx'), may hold values from -6 to 6
- segment_rows: int32 [160], replicated, may hold values from 0 to 159, each once
- step_index: int32 [1], replicated, may hold values from 10 to 13
Outputs:
- next_state: bfloat16 [4, 2048, 512], P(None, 'gy', 'gx')
Inputs may be any that keep to these rules, and one draw needn't show every extreme that they name: `segment_rows`: each strip row feeds exactly one of the 160 boundary segments.
All inputs are finite; a program needn't handle non-finite values.
Results may differ from a plain program's by a relative error of at most 0.0049.
Values may be sent and summed in bfloat16 or wider, within the bound.
A program may use at most 192 MiB of HBM per device.

v0:
```python
import functools

import jax
import jax.numpy as jnp
from jax import lax
from jax.experimental import pallas as pl
from jax.experimental.pallas import tpu as pltpu
from jax.sharding import PartitionSpec as P

SEG = 32
BAND = 8
NSTEPS = 18


SIGMA_MAX = 800.0
SIGMA_MIN = 0.002
RHO_POWER = 7.0
CHURN_GAIN = 0.25
NOISE_GAIN = 1.007
SIGMA_DATA = 0.5
RELAX_GAIN = 3.0
ROOT_HALF = 0.7071067811865476


def shifted(block, axis, step):
    count = lax.axis_size(axis)
    if step > 0:
        pairs = [(i, i + 1) for i in range(count - 1)]
    else:
        pairs = [(i + 1, i) for i in range(count - 1)]
    return lax.ppermute(block, axis, pairs)


def with_halo(net_in):
    cols = net_in.shape[2]
    left = shifted(net_in[:, :, cols - 2 :].transpose(2, 0, 1), "gx", 1)
    right = shifted(net_in[:, :, :2].transpose(2, 0, 1), "gx", -1)
    wide = jnp.concatenate(
        [left.transpose(2, 1, 0), net_in.transpose(1, 0, 2), right.transpose(2, 1, 0)], axis=2
    )
    rows = wide.shape[0]
    above = shifted(wide[rows - 2 :], "gy", 1)
    below = shifted(wide[:2], "gy", -1)
    return jnp.concatenate([above, wide, below], axis=0)


def three_parts(values):
    high = lax.reduce_precision(values, 8, 7)
    rest = values - high
    mid = lax.reduce_precision(rest, 8, 7)
    return jnp.stack([high, mid, rest - mid]).astype(jnp.bfloat16)


def bias_rows(values):
    return jnp.pad(three_parts(values), ((0, 13), (0, 0)))


def first_weights(first_kernel, first_bias, film_weight, film_bias):
    width, inner = first_kernel.shape[2], first_kernel.shape[3]
    taps = first_kernel.transpose(1, 0, 3, 2)
    conv = jnp.concatenate(
        [jnp.pad(taps, ((0, 0), (s, 1 - s), (0, 0), (0, 0))) for s in (0, 1)], axis=3
    ).reshape(12 * inner, 2 * width)
    lead = inner - film_weight.shape[1]
    film = jnp.pad(film_weight.T, ((lead, 0), (0, 0)))
    parts = [conv]
    for k in (0, 1):
        piece = film[:, k * width : (k + 1) * width]
        both = jnp.concatenate(
            [jnp.pad(piece, ((inner * (5 + s), inner * (6 - s)), (0, 0))) for s in (0, 1)], axis=1
        )
        parts.append(both)
    parts = [parts[0]] + parts[1:]
    biases = [first_bias, 1.0 + film_bias[:width], film_bias[width:]]
    row = jnp.concatenate([jnp.tile(v, 2) for v in biases])
    return jnp.concatenate([jnp.concatenate(parts, axis=1), bias_rows(row)], axis=0)


def second_weights(second_kernel):
    width, inner = second_kernel.shape[2], second_kernel.shape[3]
    taps = second_kernel.transpose(0, 1, 3, 2).reshape(3, 3 * inner, width)
    return jnp.concatenate(
        [jnp.pad(taps, ((s, 1 - s), (0, 0), (0, 0))) for s in (0, 1)], axis=2
    ).reshape(12 * inner, 2 * width)


def skip_weights(skip_kernel, second_bias):
    width, inner = skip_kernel.shape
    flat = skip_kernel.T
    both = jnp.concatenate(
        [jnp.pad(flat, ((inner * s, inner * (1 - s)), (0, 0))) for s in (0, 1)], axis=1
    )
    return jnp.concatenate([both, bias_rows(jnp.tile(second_bias, 2))], axis=0)


def out_weights(out_kernel):
    width = out_kernel.shape[1]
    return jnp.concatenate(
        [jnp.pad(out_kernel, ((0, 0), (width * s, width * (1 - s)))) for s in (0, 1)], axis=0
    )


def block_kernel(pairs, group, cols, width, net_ref, first_ref, second_ref, skip_ref, out_ref,
                 proj_ref, held):
    tile_col, tile_row = lax.axis_index("gx"), lax.axis_index("gy")
    last_col, last_row = lax.axis_size("gx") - 1, lax.axis_size("gy") - 1
    wide = net_ref.shape[2]
    place = lax.broadcasted_iota(jnp.int32, (wide, width), 0)
    low = jnp.where(tile_col == 0, 1, 0)
    high = jnp.where(tile_col == last_col, cols, cols + 1)
    col_mask = ((place >= low) & (place <= high)).astype(jnp.float32)
    ones = jnp.ones((16, wide), jnp.bfloat16)

    def hidden_pair(i, slot):
        start = pl.multiple_of(i * 32, 32)
        patch = jnp.concatenate([net_ref[b, pl.ds(start, 64), :] for b in range(3)] + [ones], axis=0)
        act = lax.dot_general(
            patch, first_ref[...], (((0,), (0,)), ((), ())), preferred_element_type=jnp.float32
        )
        for s in range(2):
            lo = s * width
            shaped = (
                act[:, lo : lo + width] * act[:, 2 * width + lo : 3 * width + lo]
                + act[:, 4 * width + lo : 5 * width + lo]
            )
            half = 0.5 * shaped
            value = half * jnp.tanh(half) + half
            if s == 0:
                inside = jnp.where((i == 0) & (tile_row == 0), 0.0, 1.0)
            else:
                inside = jnp.where((i == pairs) & (tile_row == last_row), 0.0, 1.0)
            value = value * (col_mask * inside)
            for b in range(3):
                moved = value if b == 0 else pltpu.roll(value, wide - b, 0)
                at = (s * 3 + b) * width
                held[slot, :, at : at + width] = moved[:cols].astype(jnp.bfloat16)

    def out_pair(i, slot):
        start = pl.multiple_of(i * 32 + 32, 32)
        centre = jnp.concatenate([net_ref[2, pl.ds(start, 32), :cols], ones[:, :cols]], axis=0)
        depth = 6 * width
        total = jnp.dot(held[slot], second_ref[:depth], preferred_element_type=jnp.float32)
        total += jnp.dot(held[slot + 1], second_ref[depth:], preferred_element_type=jnp.float32)
        total += lax.dot_general(
            centre, skip_ref[...], (((0,), (0,)), ((), ())), preferred_element_type=jnp.float32
        )
        branch = (total * ROOT_HALF).astype(jnp.bfloat16)
        proj_ref[i] = lax.dot_general(
            out_ref[...], branch, (((1,), (1,)), ((), ())), preferred_element_type=jnp.float32
        )

    hidden_pair(jnp.int32(0), 0)

    @pl.loop(0, pairs // group)
    def _(step):
        for k in range(group):
            hidden_pair(step * group + k + 1, k + 1)
            out_pair(step * group + k, k)
        held[0] = held[group]


def residual_block(ext, first_w, second_w, skip_w, out_w, cols):
    rows_ext, inner, cols_ext = ext.shape
    pairs = (rows_ext - 4) // 2
    width = second_w.shape[1] // 2
    wide = cols + 16
    group = 4
    flat = ext.reshape(rows_ext * inner, cols_ext)
    flat = jnp.pad(flat, ((0, 0), (0, wide + 2 - cols_ext)))
    net3 = jnp.stack([flat[:, b : b + wide] for b in range(3)])
    return pl.pallas_call(
        functools.partial(block_kernel, pairs, group, cols, width),
        out_shape=jax.ShapeDtypeStruct((pairs, out_w.shape[0], cols), jnp.float32),
        in_specs=[pl.BlockSpec(memory_space=pltpu.VMEM)] * 5,
        out_specs=pl.BlockSpec(memory_space=pltpu.VMEM),
        scratch_shapes=[pltpu.VMEM((group + 1, cols, 6 * width), jnp.bfloat16)],
        compiler_params=pltpu.CompilerParams(vmem_limit_bytes=48 * 1024 * 1024),
    )(net3, first_w, second_w, skip_w, out_w)


def noise_levels(step_index, total_steps):
    upper_root = SIGMA_MAX ** (1.0 / RHO_POWER)
    lower_root = SIGMA_MIN ** (1.0 / RHO_POWER)
    position = step_index[0].astype(jnp.float32)
    sigma_now = (upper_root + position / (total_steps - 1) * (lower_root - upper_root)) ** RHO_POWER
    sigma_next = (
        upper_root + (position + 1.0) / (total_steps - 1) * (lower_root - upper_root)
    ) ** RHO_POWER
    return (sigma_now, sigma_next)


def sampler_terms(step_index):
    sigma_now, sigma_next = noise_levels(step_index, NSTEPS)
    sigma_hat = (1.0 + CHURN_GAIN) * sigma_now
    spread = NOISE_GAIN * jnp.sqrt(sigma_hat * sigma_hat - sigma_now * sigma_now)
    energy = sigma_hat * sigma_hat + SIGMA_DATA * SIGMA_DATA
    scale_in = 1.0 / jnp.sqrt(energy)
    scale_skip = SIGMA_DATA * SIGMA_DATA / energy
    scale_out = sigma_hat * SIGMA_DATA / jnp.sqrt(energy)
    stride = (sigma_next - sigma_hat) / sigma_hat
    return (spread, scale_in, scale_skip, scale_out, stride)


def relax_weight(distance, band):
    return jnp.where(
        (distance >= 0) & (distance < band), RELAX_GAIN * (band - distance) / band, 0.0
    )


def side_values(table, first_seg, seg_total, length):
    chosen = table[first_seg : first_seg + seg_total]
    return chosen.transpose(1, 2, 0, 3).reshape(table.shape[1], table.shape[2], length)


def boundary_ids(col_ids, row_ids, col_count, row_count, segs_wide, segs_tall, segment_rows):
    seg_total = segment_rows.shape[0]
    along_wide = jnp.arange(segs_wide, dtype=jnp.int32)[None, :]
    along_tall = jnp.arange(segs_tall, dtype=jnp.int32)[None, :]
    wide_all = col_count * segs_wide
    tall_all = row_count * segs_tall
    south_segs = col_ids[:, None] * segs_wide + along_wide
    north_segs = wide_all + col_ids[:, None] * segs_wide + along_wide
    west_segs = 2 * wide_all + row_ids[:, None] * segs_tall + along_tall
    east_segs = 2 * wide_all + tall_all + row_ids[:, None] * segs_tall + along_tall
    seg_ids = jnp.concatenate([south_segs, north_segs, west_segs, east_segs], axis=1)
    valid = jnp.concatenate(
        [
            jnp.broadcast_to((row_ids == 0)[:, None], south_segs.shape),
            jnp.broadcast_to((row_ids == row_count - 1)[:, None], north_segs.shape),
            jnp.broadcast_to((col_ids == 0)[:, None], west_segs.shape),
            jnp.broadcast_to((col_ids == col_count - 1)[:, None], east_segs.shape),
        ],
        axis=1,
    )
    matches = seg_ids[:, :, None] == jnp.arange(seg_total, dtype=jnp.int32)[None, None, :]
    looked_up = jnp.sum(jnp.where(matches, segment_rows[None, None, :], 0), axis=2)
    return jnp.where(valid, looked_up, -1).reshape(-1)


def on_device(
    noisy_state,
    fresh_noise,
    conditioning,
    first_kernel,
    first_bias,
    film_weight,
    film_bias,
    second_kernel,
    second_bias,
    skip_kernel,
    out_kernel,
    strip_table,
    segment_rows,
    step_index,
):
    tile_col = lax.axis_index("gx")
    tile_row = lax.axis_index("gy")
    col_count = lax.axis_size("gx")
    row_count = lax.axis_size("gy")
    channels, tile_rows, tile_cols = noisy_state.shape
    total_rows = tile_rows * row_count
    total_cols = tile_cols * col_count
    spread, scale_in, scale_skip, scale_out, stride = sampler_terms(step_index)
    segs_wide = tile_cols // SEG
    segs_tall = tile_rows // SEG
    slot_count = 2 * (segs_wide + segs_tall)
    wanted = boundary_ids(
        jnp.reshape(tile_col, (1,)),
        jnp.reshape(tile_row, (1,)),
        col_count,
        row_count,
        segs_wide,
        segs_tall,
        segment_rows,
    )
    shard_rows = lax.all_gather(strip_table, "gx", axis=0, tiled=True)
    chosen = (wanted[:, None] == jnp.arange(shard_rows.shape[0], dtype=jnp.int32)[None, :]).astype(
        jnp.bfloat16
    )
    delivered = jnp.dot(chosen, shard_rows, preferred_element_type=jnp.float32)
    table = delivered.reshape(slot_count, channels, BAND, SEG)
    south_side = side_values(table, 0, segs_wide, tile_cols)
    north_side = side_values(table, segs_wide, segs_wide, tile_cols)
    west_side = side_values(table, 2 * segs_wide, segs_tall, tile_rows)
    east_side = side_values(table, 2 * segs_wide + segs_tall, segs_tall, tile_rows)
    state_hat = noisy_state.astype(jnp.float32) + spread * fresh_noise.astype(jnp.float32)
    net_in = jnp.concatenate(
        [scale_in * state_hat, conditioning.astype(jnp.float32)], axis=0
    ).astype(jnp.bfloat16)
    ext = with_halo(net_in)
    pairs_out = residual_block(
        ext,
        first_weights(first_kernel, first_bias, film_weight, film_bias),
        second_weights(second_kernel),
        skip_weights(skip_kernel, second_bias),
        out_weights(out_kernel),
        tile_cols,
    )
    projected = pairs_out.reshape(tile_rows // 2, 2, channels, tile_cols)
    projected = projected.transpose(2, 0, 1, 3).reshape(channels, tile_rows, tile_cols)
    denoised = scale_skip * state_hat + scale_out * projected
    global_rows = (tile_row * tile_rows + jnp.arange(tile_rows, dtype=jnp.int32)).astype(
        jnp.float32
    )
    global_cols = (tile_col * tile_cols + jnp.arange(tile_cols, dtype=jnp.int32)).astype(
        jnp.float32
    )
    south_weight = relax_weight(global_rows, BAND)
    north_weight = relax_weight(total_rows - 1.0 - global_rows, BAND)
    west_weight = relax_weight(global_cols, BAND)
    east_weight = relax_weight(total_cols - 1.0 - global_cols, BAND)
    rest_rows = tile_rows - BAND
    rest_cols = tile_cols - BAND
    south_full = jnp.pad(south_side, ((0, 0), (0, rest_rows), (0, 0)))
    north_full = jnp.pad(north_side[:, ::-1, :], ((0, 0), (rest_rows, 0), (0, 0)))
    west_full = jnp.pad(west_side.transpose(0, 2, 1), ((0, 0), (0, 0), (0, rest_cols)))
    east_full = jnp.pad(east_side.transpose(0, 2, 1)[:, :, ::-1], ((0, 0), (0, 0), (rest_cols, 0)))
    numerator = (
        denoised
        + south_weight[None, :, None] * south_full
        + north_weight[None, :, None] * north_full
    )
    numerator = (
        numerator + west_weight[None, None, :] * west_full + east_weight[None, None, :] * east_full
    )
    denominator = (
        1.0 + south_weight[:, None] + north_weight[:, None] + (west_weight + east_weight)[None, :]
    )
    relaxed = numerator / denominator[None]
    return (state_hat + stride * (state_hat - relaxed)).astype(jnp.bfloat16)


def solution(mesh):
    return jax.shard_map(
        on_device,
        mesh=mesh,
        in_specs=(
            P(None, "gy", "gx"),
            P(None, "gy", "gx"),
            P(None, "gy", "gx"),
            P(),
            P(),
            P(),
            P(),
            P(),
            P(),
            P(),
            P(),
            P("gx", None),
            P(),
            P(),
        ),
        out_specs=P(None, "gy", "gx"),
        check_vma=False,
    )
```

profile of v0, /device:TPU:1, one launch (start us, length us, event | category | flops | bytes accessed | tf_op | source)
XLA Modules:
  0.0 140.4 jit_solution(8843513489602907115)
XLA Ops:
  0.8 1.1 multiply_convert_fusion
  2.0 0.2 copy.66
  2.2 2.0 %copy.67 = bf16[12,256,128]{1,0,2:T(8,128)(2,1)S(1)} copy(bf16[12,256,128]{2,1,0:T(8,128)(2,1)} %param.16) | data formatting | bytes 1572864 | tf_op args[2]
  4.2 0.0 copy-start.5
  4.2 0.0 copy-start.10
  4.2 0.0 copy-start.11
  4.2 0.0 copy-start.13
  4.2 0.0 copy-start.7
  4.2 0.0 copy-start.6
  4.3 0.0 copy-start.14
  4.3 4.1 %collective-permute-start = (bf16[2,16,256]{2,1,0:T(8,128)(2,1)S(1)}, bf16[2,16,256]{2,1,0:T(8,128)(2,1)S(1)}, u32[]{:S(2)}, u32[]{:S(2)}) collective-permute-start(bf16[2,16,256]{2,1,0:T(8,128)(2,1)S(1)} %get-tuple-element.10), channel_id=1, source_target_pairs={{0,8},{8,16},{16,24},{1,9},{9,17},{17,25},{2,10},{10,18},{18,26},{... | collective-permute-start | bytes 49160 | tf_op jit(solution)/shard_map/ppermute | solution.py:31
  8.4 0.0 copy-start.4
  8.4 1.4 %collective-permute-start.1 = (bf16[2,16,256]{2,1,0:T(8,128)(2,1)S(1)}, bf16[2,16,256]{2,1,0:T(8,128)(2,1)S(1)}, u32[]{:S(2)}, u32[]{:S(2)}) collective-permute-start(bf16[2,16,256]{2,1,0:T(8,128)(2,1)S(1)} %get-tuple-element.11), channel_id=1, source_target_pairs={{8,0},{16,8},{24,16},{9,1},{17,9},{25,17},{10,2},{18,10},{26,18},{... | collective-permute-start | bytes 49160 | tf_op jit(solution)/shard_map/ppermute | solution.py:31
  9.8 0.5 fusion.2
  10.3 0.0 copy-start.9
  10.4 0.0 copy-start.8
  10.4 0.0 copy-done.5
  10.4 9.0 %all_gather.3 = bf16[160,1024]{1,0:T(8,128)(2,1)S(1)} all-gather(bf16[40,1024]{1,0:T(8,128)(2,1)S(1)} %copy-done.5), channel_id=1, replica_groups=mesh['gx'=4,'gy'=8] {'gx'}, dimensions={0}, use_global_device_ids=true | all-gather | bytes 409600 | tf_op jit(solution)/shard_map/all_gather | solution.py:276
  19.4 0.1 add_bitcast_fusion
  19.5 0.0 copy-done.10
  19.5 0.2 select_reduce_fusion
  19.8 0.1 add_select_fusion
  19.8 0.2 fusion.20
  20.1 0.0 copy-done.11
  20.1 0.0 copy-done.13
  20.2 0.0 copy-done.7
  20.4 0.0 copy-done.4
  20.4 0.2 copy.74
  20.6 0.1 fusion.3
  20.8 0.1 broadcast_add_fusion
  21.0 0.0 collective-permute-done
  21.0 0.0 collective-permute-done.1
  21.0 0.1 pad_maximum_fusion.3
  21.1 0.3 fusion.37
  21.4 0.5 copy.68
  21.9 6.8 %collective-permute-start.2 = (bf16[2,16,132]{2,1,0:T(8,128)(2,1)S(1)}, bf16[2,16,132]{2,1,0:T(8,128)(2,1)S(1)}, u32[]{:S(2)}, u32[]{:S(2)}) collective-permute-start(bf16[2,16,132]{2,1,0:T(8,128)(2,1)S(1)} %copy.68), channel_id=1, source_target_pairs={{0,1},{1,2},{2,3},{3,4},{4,5},{5,6},{6,7},{8,9},{9,10},{10,11},{11... | collective-permute-start | bytes 25352 | tf_op jit(solution)/shard_map/ppermute | solution.py:31
  28.7 0.5 copy.69
  29.3 1.9 %collective-permute-start.3 = (bf16[2,16,132]{2,1,0:T(8,128)(2,1)S(1)}, bf16[2,16,132]{2,1,0:T(8,128)(2,1)}, u32[]{:S(2)}, u32[]{:S(2)}) collective-permute-start(bf16[2,16,132]{2,1,0:T(8,128)(2,1)S(1)} %copy.69), channel_id=1, source_target_pairs={{1,0},{2,1},{3,2},{4,3},{5,4},{6,5},{7,6},{9,8},{10,9},{11,10},{12... | collective-permute-start | bytes 25352 | tf_op jit(solution)/shard_map/ppermute | solution.py:31
  31.2 0.5 and_select_fusion
  31.8 0.1 slice.75
  31.9 0.2 copy.79
  32.1 3.0 %rev.7 = f32[4,256,8]{2,1,0:T(8,128)} reverse(f32[4,256,8]{2,1,0:T(8,128)S(1)} %bitcast.50), dimensions={2} | reverse | bytes 65536 | tf_op jit(solution)/shard_map/rev | solution.py:317
  35.1 0.1 slice.73
  35.2 1.0 copy.78
  36.2 0.1 slice.71
  36.4 0.1 reshape.535
  36.5 0.1 slice.69
  36.6 0.1 reshape.534
  36.8 0.0 collective-permute-done.2
  36.8 0.6 copy.70
  37.4 0.0 collective-permute-done.3
  37.4 1.3 copy.71
  38.7 2.2 %pad_maximum_fusion.1 = bf16[260,16,132]{0,1,2:T(8,128)(2,1)} fusion(bf16[2,16,132]{0,1,2:T(8,128)(2,1)S(1)} %copy.71, bf16[256,16,2]{0,1,2:T(8,128)(2,1)S(1)} %bitcast.63, bf16[256,16,128]{0,1,2:T(8,128)(2,1)S(1)} %fusion.2, bf16[256,16,2]{0,1,2:T(8,128)(2,1)S(1)} %bitcast.61, bf16[2,16,132]{0,1,2:T(8,128)(2,1)S(1)} %copy.70), kind=kLoop, calls=%fused_computation.4 | loop fusion | flops 5491200 | bytes 2196480 | tf_op jit(solution)/shard_map/concatenate | solution.py:44
  40.9 4.3 %copy.72 = bf16[260,16,132]{2,1,0:T(8,128)(2,1)S(1)} copy(bf16[260,16,132]{0,1,2:T(8,128)(2,1)} %pad_maximum_fusion.1) | data formatting | bytes 2196480 | tf_op jit(solution)/shard_map/concatenate | solution.py:44
  45.2 1.9 %slice_bitcast_fusion.2 = (bf16[1,4160,144]{2,1,0:T(8,128)(2,1)S(1)}, bf16[1,4160,144]{2,1,0:T(8,128)(2,1)S(1)}, bf16[1,4160,144]{2,1,0:T(8,128)(2,1)S(1)}) fusion(bf16[4160,132]{1,0:T(8,128)(2,1)S(1)} %bitcast.49), kind=kLoop, calls=%fused_computation.3 | loop fusion | bytes 4692480 | tf_op jit(solution)/shard_map/stack | solution.py:170
  47.2 3.6 %pad_maximum_fusion.net_ref = bf16[3,4160,144]{2,1,0:T(8,128)(2,1)} fusion(bf16[1,4160,144]{2,1,0:T(8,128)(2,1)S(1)} %get-tuple-element.9, bf16[1,4160,144]{2,1,0:T(8,128)(2,1)S(1)} %get-tuple-element.8, bf16[1,4160,144]{2,1,0:T(8,128)(2,1)S(1)} %get-tuple-element.7), kind=kLoop, calls=%fused_computation | loop fusion | flops 3594240 | bytes 7188480 | tf_op jit(solution)/shard_map/stack | solution.py:170
  50.8 87.2 %shard_map.136 = f32[128,8,128]{2,1,0:T(8,128)S(1)} custom-call(bf16[3,4160,144]{2,1,0:T(8,128)(2,1)} %pad_maximum_fusion.net_ref, bf16[208,768]{1,0:T(8,128)(2,1)S(1)} %pad_maximum_fusion.4.first_ref, bf16[1536,256]{1,0:T(8,128)(2,1)S(1)} %bitcast.48, bf16[48,256]{1,0:T(8,128)(2,1)S(1)} %fusion.17.skip_ref, bf16[8,256]{1,0:T(8,128)(2,1)S(1)} %fusion.33.out_ref), custom_call_target="tpu_custom_call" | custom-call | tf_op jit(solution)/shard_map/pallas_call | solution.py:171
  138.0 0.0 copy-start.3
  138.0 0.3 copy.75
  138.3 0.7 copy-done
  139.0 0.2 copy-done.1
  139.2 0.1 copy-done.2
  139.3 0.1 copy-done.3
  139.3 1.1 add_convert_fusion
  (46 shorter events, 0.5 us)
Async XLA Ops:
  4.2 6.3 %copy-start.5 = (bf16[40,1024]{1,0:T(8,128)(2,1)S(1)}, bf16[40,1024]{1,0:T(8,128)(2,1)}, u32[]{:S(2)}) copy-start(bf16[40,1024]{1,0:T(8,128)(2,1)} %param.25) | copy-start | bytes 245764
  4.2 15.4 %copy-start.10 = (s32[160]{0:T(256)S(1)}, s32[160]{0:T(256)}, u32[]{:S(2)}) copy-start(s32[160]{0:T(256)} %param.26) | copy-start | bytes 1924
  4.2 15.9 %copy-start.11 = (f32[256]{0:T(256)S(1)}, f32[256]{0:T(256)}, u32[]{:S(2)}) copy-start(f32[256]{0:T(256)} %param.20) | copy-start | bytes 3076
  4.2 15.9 %copy-start.13 = (f32[128]{0:T(128)S(1)}, f32[128]{0:T(128)}, u32[]{:S(2)}) copy-start(f32[128]{0:T(128)} %param.18) | copy-start | bytes 1540
  4.2 16.0 %copy-start.7 = (bf16[256,12]{0,1:T(8,128)(2,1)S(1)}, bf16[256,12]{0,1:T(8,128)(2,1)}, u32[]{:S(2)}) copy-start(bf16[256,12]{0,1:T(8,128)(2,1)} %param.19) | copy-start | bytes 18436
  4.2 16.0 %copy-start.6 = (bf16[3,3,128,16]{2,3,1,0:T(8,128)(2,1)S(1)}, bf16[3,3,128,16]{2,3,1,0:T(8,128)(2,1)}, u32[]{:S(2)}) copy-start(bf16[3,3,128,16]{2,3,1,0:T(8,128)(2,1)} %param.17) | copy-start | bytes 110596
  4.3 16.1 %copy-start.14 = (f32[128]{0:T(128)S(1)}, f32[128]{0:T(128)}, u32[]{:S(2)}) copy-start(f32[128]{0:T(128)} %param.22) | copy-start | bytes 1540
  4.3 16.7 %collective-permute-start = (bf16[2,16,256]{2,1,0:T(8,128)(2,1)S(1)}, bf16[2,16,256]{2,1,0:T(8,128)(2,1)S(1)}, u32[]{:S(2)}, u32[]{:S(2)}) collective-permute-start(bf16[2,16,256]{2,1,0:T(8,128)(2,1)S(1)} %get-tuple-element.10), channel_id=1, source_target_pairs={{0,8},{8,16},{16,24},{1,9},{9,17},{17,25},{2,10},{10,18},{18,26},{... | collective-permute-start | bytes 49160 | tf_op jit(solution)/shard_map/ppermute | solution.py:31
  8.4 12.0 %copy-start.4 = (bf16[3,3,128,128]{3,2,1,0:T(8,128)(2,1)S(1)}, bf16[3,3,128,128]{3,2,1,0:T(8,128)(2,1)}, u32[]{:S(2)}) copy-start(bf16[3,3,128,128]{3,2,1,0:T(8,128)(2,1)} %param.21) | copy-start | bytes 884740
  8.4 12.6 %collective-permute-start.1 = (bf16[2,16,256]{2,1,0:T(8,128)(2,1)S(1)}, bf16[2,16,256]{2,1,0:T(8,128)(2,1)S(1)}, u32[]{:S(2)}, u32[]{:S(2)}) collective-permute-start(bf16[2,16,256]{2,1,0:T(8,128)(2,1)S(1)} %get-tuple-element.11), channel_id=1, source_target_pairs={{8,0},{16,8},{24,16},{9,1},{17,9},{25,17},{10,2},{18,10},{26,18},{... | collective-permute-start | bytes 49160 | tf_op jit(solution)/shard_map/ppermute | solution.py:31
  10.3 10.3 %copy-start.9 = (bf16[4,128]{1,0:T(4,128)(2,1)S(1)}, bf16[4,128]{1,0:T(4,128)(2,1)}, u32[]{:S(2)}) copy-start(bf16[4,128]{1,0:T(4,128)(2,1)} %param.24) | copy-start | bytes 3076
  10.4 10.4 %copy-start.8 = (bf16[128,16]{0,1:T(8,128)(2,1)S(1)}, bf16[128,16]{0,1:T(8,128)(2,1)}, u32[]{:S(2)}) copy-start(bf16[128,16]{0,1:T(8,128)(2,1)} %param.23) | copy-start | bytes 12292
  21.9 14.9 %collective-permute-start.2 = (bf16[2,16,132]{2,1,0:T(8,128)(2,1)S(1)}, bf16[2,16,132]{2,1,0:T(8,128)(2,1)S(1)}, u32[]{:S(2)}, u32[]{:S(2)}) collective-permute-start(bf16[2,16,132]{2,1,0:T(8,128)(2,1)S(1)} %copy.68), channel_id=1, source_target_pairs={{0,1},{1,2},{2,3},{3,4},{4,5},{5,6},{6,7},{8,9},{9,10},{10,11},{11... | collective-permute-start | bytes 25352 | tf_op jit(solution)/shard_map/ppermute | solution.py:31
  29.3 8.1 %collective-permute-start.3 = (bf16[2,16,132]{2,1,0:T(8,128)(2,1)S(1)}, bf16[2,16,132]{2,1,0:T(8,128)(2,1)}, u32[]{:S(2)}, u32[]{:S(2)}) collective-permute-start(bf16[2,16,132]{2,1,0:T(8,128)(2,1)S(1)} %copy.69), channel_id=1, source_target_pairs={{1,0},{2,1},{3,2},{4,3},{5,4},{6,5},{7,6},{9,8},{10,9},{11,10},{12... | collective-permute-start | bytes 25352 | tf_op jit(solution)/shard_map/ppermute | solution.py:31
  50.8 87.5 %copy-start.12 = (f32[128]{0:T(128)S(1)}, f32[128]{0:T(128)}, u32[]{:S(2)}) copy-start(f32[128]{0:T(128)} %get-tuple-element.32) | copy-start | bytes 1540
  138.0 1.1 copy-start
  138.0 1.2 copy-start.1
  138.0 1.3 copy-start.2
  138.0 1.3 copy-start.3
where the time goes:
time: 141 us; the launch traced here: 140 us
  Pallas kernels  87.2 us (62%)
  local copies, waits for them, and re-layouts  18.2 us (13%)
  starting transfers between devices  14.2 us (10%)
  other arithmetic  10 us (7%)
  blocking collectives  9.02 us (6%)
  between operations  1.62 us (1%)
    pallas_call x1, Pallas kernels, residual_block(): pl.pallas_call(functools.partial(block_kernel, pairs, group, cols, width)...  87.2 us
    ppermute x4, starting transfers between devices, shifted(): return lax.ppermute(block, axis, pairs)  14.2 us
    all_gather x1, blocking collectives, on_device(): shard_rows = lax.all_gather(strip_table, 'gx', axis=0, tiled=True)  9.02 us
    concatenate x1, local copies, waits for them, and re-layouts, with_halo(): return jnp.concatenate([above, wide, below], axis=0)  4.27 us
    another operation x1, other arithmetic, residual_block(): net3 = jnp.stack([flat[:, b:b + wide] for b in range(3)])  3.63 us
    unnamed x36, local copies, waits for them, and re-layouts  3.35 us
    rev x1, local copies, waits for them, and re-layouts, on_device(): east_side.transpose(0, 2, 1)[:, :, ::-1]  2.99 us
  transfers between devices with their start and end apart: 4, of which 0 were waited for; matrix products, arithmetic and copies ran while one was open for 6% of the time, Pallas kernels for 0%

commit v1 on v0

--- a/solution.py
+++ b/solution.py
@@ -19,6 +19,7 @@
 NOISE_GAIN = 1.007
 SIGMA_DATA = 0.5
 RELAX_GAIN = 3.0
+SUB = 4
 ROOT_HALF = 0.7071067811865476
 
 
@@ -31,17 +32,15 @@
     return lax.ppermute(block, axis, pairs)
 
 
-def with_halo(net_in):
-    cols = net_in.shape[2]
+def halos(net_in):
+    channels, rows, cols = net_in.shape
     left = shifted(net_in[:, :, cols - 2 :].transpose(2, 0, 1), "gx", 1)
     right = shifted(net_in[:, :, :2].transpose(2, 0, 1), "gx", -1)
-    wide = jnp.concatenate(
-        [left.transpose(2, 1, 0), net_in.transpose(1, 0, 2), right.transpose(2, 1, 0)], axis=2
-    )
-    rows = wide.shape[0]
-    above = shifted(wide[rows - 2 :], "gy", 1)
-    below = shifted(wide[:2], "gy", -1)
-    return jnp.concatenate([above, wide, below], axis=0)
+    gap = jnp.zeros((channels, rows, cols - 4), net_in.dtype)
+    beside = jnp.concatenate([right.transpose(1, 2, 0), gap, left.transpose(1, 2, 0)], axis=2)
+    tail = jnp.concatenate([net_in[:, rows - 2 :], beside[:, rows - 2 :]], axis=2)
+    head = jnp.concatenate([net_in[:, :2], beside[:, :2]], axis=2)
+    return beside, shifted(tail, "gy", 1), shifted(head, "gy", -1)
 
 
 def three_parts(values):
@@ -100,23 +99,50 @@
     )
 
 
-def block_kernel(pairs, group, cols, width, net_ref, first_ref, second_ref, skip_ref, out_ref,
-                 proj_ref, held):
+def block_kernel(pairs, group, cols, width, main_ref, side_ref, above_ref, below_ref, first_ref,
+                 second_ref, out_ref, proj_ref, net_ref, edge_ref, held, patches):
     tile_col, tile_row = lax.axis_index("gx"), lax.axis_index("gy")
     last_col, last_row = lax.axis_size("gx") - 1, lax.axis_size("gy") - 1
-    wide = net_ref.shape[2]
+    wide = cols + 16
+    inner, rows = main_ref.shape[0], main_ref.shape[1]
+    for c in range(inner):
+        spot = pl.ds(2 * inner + c, rows, stride=inner)
+        net_ref[spot] = main_ref[c].astype(jnp.float32)
+        edge_ref[spot] = side_ref[c].astype(jnp.float32)
+        upper, lower = above_ref[c].astype(jnp.float32), below_ref[c].astype(jnp.float32)
+        for r in range(2):
+            at, end = r * inner + c, (rows + 2 + r) * inner + c
+            net_ref[at : at + 1] = upper[r : r + 1, :cols]
+            edge_ref[at : at + 1] = upper[r : r + 1, cols:]
+            net_ref[end : end + 1] = lower[r : r + 1, :cols]
+            edge_ref[end : end + 1] = lower[r : r + 1, cols:]
     place = lax.broadcasted_iota(jnp.int32, (wide, width), 0)
     low = jnp.where(tile_col == 0, 1, 0)
     high = jnp.where(tile_col == last_col, cols, cols + 1)
     col_mask = ((place >= low) & (place <= high)).astype(jnp.float32)
     ones = jnp.ones((16, wide), jnp.bfloat16)
-
-    def hidden_pair(i, slot):
-        start = pl.multiple_of(i * 32, 32)
-        patch = jnp.concatenate([net_ref[b, pl.ds(start, 64), :] for b in range(3)] + [ones], axis=0)
-        act = lax.dot_general(
-            patch, first_ref[...], (((0,), (0,)), ((), ())), preferred_element_type=jnp.float32
-        )
+    depth = 6 * width
+
+    def moved_lanes(x, step):
+        return (pltpu.roll(x, step, 1) if step else x).astype(jnp.bfloat16)
+
+    def hidden_pairs(first, count, slot):
+        for k in range(count):
+            start = pl.multiple_of((first + k) * 32, 32)
+            x = jnp.concatenate([net_ref[pl.ds(start, 64)], edge_ref[pl.ds(start, 64)]], axis=1)
+            patch = jnp.concatenate([moved_lanes(x, 2 - b)[:, :wide] for b in range(3)] + [ones], axis=0)
+            patches[k * wide : (k + 1) * wide] = patch.T
+        for top in range(0, count, SUB):
+            size = min(SUB, count - top)
+            acts = jnp.dot(
+                patches[top * wide : (top + size) * wide],
+                first_ref[...],
+                preferred_element_type=jnp.float32,
+            )
+            for k in range(size):
+                activate(acts[k * wide : (k + 1) * wide], first + top + k, slot + top + k)
+
+    def activate(act, i, slot):
         for s in range(2):
             lo = s * width
             shaped = (
@@ -132,50 +158,62 @@
             value = value * (col_mask * inside)
             for b in range(3):
                 moved = value if b == 0 else pltpu.roll(value, wide - b, 0)
+                moved = moved[:cols].astype(jnp.bfloat16)
                 at = (s * 3 + b) * width
-                held[slot, :, at : at + width] = moved[:cols].astype(jnp.bfloat16)
-
-    def out_pair(i, slot):
-        start = pl.multiple_of(i * 32 + 32, 32)
-        centre = jnp.concatenate([net_ref[2, pl.ds(start, 32), :cols], ones[:, :cols]], axis=0)
-        depth = 6 * width
-        total = jnp.dot(held[slot], second_ref[:depth], preferred_element_type=jnp.float32)
-        total += jnp.dot(held[slot + 1], second_ref[depth:], preferred_element_type=jnp.float32)
-        total += lax.dot_general(
-            centre, skip_ref[...], (((0,), (0,)), ((), ())), preferred_element_type=jnp.float32
+                held[slot, :, at : at + width] = moved
+                if slot > 0:
+                    held[slot - 1, :, depth + at : depth + at + width] = moved
+
+    def out_pairs(first):
+        for k in range(group):
+            start = pl.multiple_of((first + k) * 32 + 32, 32)
+            x = net_ref[pl.ds(start, 32)].astype(jnp.bfloat16)
+            centre = jnp.concatenate([x, ones[:, :cols]], axis=0)
+            held[k, :, 2 * depth :] = centre.T
+        total = jnp.dot(
+            held[:group].reshape(group * cols, second_ref.shape[0]),
+            second_ref[...],
+            preferred_element_type=jnp.float32,
         )
         branch = (total * ROOT_HALF).astype(jnp.bfloat16)
-        proj_ref[i] = lax.dot_general(
-            out_ref[...], branch, (((1,), (1,)), ((), ())), preferred_element_type=jnp.float32
-        )
-
-    hidden_pair(jnp.int32(0), 0)
+        for k in range(group):
+            proj_ref[first + k] = lax.dot_general(
+                out_ref[...],
+                branch[k * cols : (k + 1) * cols],
+                (((1,), (1,)), ((), ())),
+                preferred_element_type=jnp.float32,
+            )
+
+    hidden_pairs(jnp.int32(0), 1, 0)
 
     @pl.loop(0, pairs // group)
     def _(step):
-        for k in range(group):
-            hidden_pair(step * group + k + 1, k + 1)
-            out_pair(step * group + k, k)
-        held[0] = held[group]
-
-
-def residual_block(ext, first_w, second_w, skip_w, out_w, cols):
-    rows_ext, inner, cols_ext = ext.shape
-    pairs = (rows_ext - 4) // 2
+        hidden_pairs(step * group + 1, group, 1)
+        out_pairs(step * group)
+        held[0, :, :depth] = held[group, :, :depth]
+
+
+def residual_block(net_in, beside, above, below, first_w, second_w, skip_w, out_w):
+    inner, rows, cols = net_in.shape
+    pairs = rows // 2
     width = second_w.shape[1] // 2
+    second_w = jnp.concatenate([second_w, skip_w], axis=0)
     wide = cols + 16
-    group = 4
-    flat = ext.reshape(rows_ext * inner, cols_ext)
-    flat = jnp.pad(flat, ((0, 0), (0, wide + 2 - cols_ext)))
-    net3 = jnp.stack([flat[:, b : b + wide] for b in range(3)])
+    group = 16
     return pl.pallas_call(
         functools.partial(block_kernel, pairs, group, cols, width),
         out_shape=jax.ShapeDtypeStruct((pairs, out_w.shape[0], cols), jnp.float32),
-        in_specs=[pl.BlockSpec(memory_space=pltpu.VMEM)] * 5,
+        in_specs=[pl.BlockSpec(memory_space=pltpu.VMEM)] * 7,
         out_specs=pl.BlockSpec(memory_space=pltpu.VMEM),
-        scratch_shapes=[pltpu.VMEM((group + 1, cols, 6 * width), jnp.bfloat16)],
+        scratch_shapes=[
+            pltpu.VMEM(((rows + 4) * inner, cols), jnp.float32),
+            pltpu.VMEM(((rows + 4) * inner, cols), jnp.float32),
+            pltpu.VMEM((group + 1, cols, second_w.shape[0]), jnp.bfloat16),
+            pltpu.VMEM((group * wide, first_w.shape[0]), jnp.bfloat16),
+        ],
         compiler_params=pltpu.CompilerParams(vmem_limit_bytes=48 * 1024 * 1024),
-    )(net3, first_w, second_w, skip_w, out_w)
+        cost_estimate=pl.CostEstimate(flops=20_000_000_000, bytes_accessed=8_000_000, transcendentals=4_500_000),
+    )(net_in, beside, above, below, first_w, second_w, out_w)
 
 
 def noise_levels(step_index, total_steps):
@@ -287,14 +325,13 @@
     net_in = jnp.concatenate(
         [scale_in * state_hat, conditioning.astype(jnp.float32)], axis=0
     ).astype(jnp.bfloat16)
-    ext = with_halo(net_in)
     pairs_out = residual_block(
-        ext,
+        net_in,
+        *halos(net_in),
         first_weights(first_kernel, first_bias, film_weight, film_bias),
         second_weights(second_kernel),
         skip_weights(skip_kernel, second_bias),
         out_weights(out_kernel),
-        tile_cols,
     )
     projected = pairs_out.reshape(tile_rows // 2, 2, channels, tile_cols)
     projected = projected.transpose(2, 0, 1, 3).reshape(channels, tile_rows, tile_cols)

time: 141 us -> 91.1 us (0.65)
  Pallas kernels: 87.2 us -> 40.6 us
  other arithmetic: 10 us -> 7.41 us
    pallas_call x1, Pallas kernels: 87.2 us -> 40.6 us  [residual_block(): pl.pallas_call(functools.partial(block_kernel, pairs, group, cols, width)...]
    slice x6 -> x10, local copies, waits for them, and re-layouts: 0.38 us -> 6 us  [side_values(): chosen = table[first_seg:first_seg + seg_total]]
    concatenate x1, local copies, waits for them, and re-layouts: 4.27 us -> 0.08 us  [halos(): jnp.concatenate([right.transpose(1, 2, 0), gap, left.transpose(1, 2, 0)],...]
    another operation x5 -> x4, other arithmetic: 4.8 us -> 1.17 us  [the longest x1 3.63 us: residual_block(): net3 = jnp.stack([flat[:, b:b + wide] for b in range(3)])]
    another operation x2 -> x0, local copies, waits for them, and re-layouts: 2.12 us -> none  [the longest x1 1.93 us: residual_block(): net3 = jnp.stack([flat[:, b:b + wide] for b in range(3)])]
    rev x1, local copies, waits for them, and re-layouts: 2.99 us -> 5.02 us  [on_device(): east_side.transpose(0, 2, 1)[:, :, ::-1]]
    concatenate x3 -> x6, other arithmetic: 2.4 us -> 3.59 us  [the longest x1 2.19 us: halos(): jnp.concatenate([right.transpose(1, 2, 0), gap, left.transpose(1, 2, 0)],...]
    unnamed x36 -> x37, local copies, waits for them, and re-layouts: 3.35 us -> 2.4 us
  transfers between devices with their start and end apart: 4 -> 4, of which waited for: 0 -> 0; matrix products, arithmetic and copies ran while one was open for 6% -> 17% of each run, Pallas kernels for 0% -> 0%
where the time goes in v1:
time: 91.1 us; the launch traced here: 90.3 us
  Pallas kernels  40.6 us (45%)
  local copies, waits for them, and re-layouts  17.6 us (19%)
  starting transfers between devices  14.5 us (16%)
  blocking collectives  8.35 us (9%)
  other arithmetic  7.41 us (8%)
  between operations  1.58 us (2%)
    pallas_call x1, Pallas kernels, residual_block(): pl.pallas_call(functools.partial(block_kernel, pairs, group, cols, width)...  40.6 us
    ppermute x4, starting transfers between devices, shifted(): return lax.ppermute(block, axis, pairs)  14.5 us
    all_gather x1, blocking collectives, on_device(): shard_rows = lax.all_gather(strip_table, 'gx', axis=0, tiled=True)  8.35 us
    slice x10, local copies, waits for them, and re-layouts, side_values(): chosen = table[first_seg:first_seg + seg_total]  6 us
    rev x1, local copies, waits for them, and re-layouts, on_device(): east_side.transpose(0, 2, 1)[:, :, ::-1]  5.02 us
    ppermute x2, local copies, waits for them, and re-layouts, shifted(): return lax.ppermute(block, axis, pairs)  2.79 us
    unnamed x37, local copies, waits for them, and re-layouts  2.4 us
    concatenate x1, other arithmetic, halos(): jnp.concatenate([right.transpose(1, 2, 0), gap, left.transpose(1, 2, 0)],...  2.19 us
  transfers between devices with their start and end apart: 4, of which 0 were waited for; matrix products, arithmetic and copies ran while one was open for 17% of the time, Pallas kernels for 0%

profile of v1, /device:TPU:1, one launch (start us, length us, event | category | flops | bytes accessed | tf_op | source)
XLA Modules:
  0.0 90.3 jit_solution(5941246688376893255)
XLA Ops:
  0.9 1.1 %multiply_convert_fusion = bf16[4,256,128]{2,1,0:T(8,128)(2,1)S(1)} fusion(bf16[4,256,128]{2,1,0:T(8,128)(2,1)} %param.15, bf16[4,256,128]{2,1,0:T(8,128)(2,1)} %param.14, f32[]{:T(128)S(6)} %div.41, f32[]{:T(128)S(6)} %mul_shard_map.6), kind=kLoop, calls=%fused_computation.34 | loop fusion | flops 786432 | bytes 786440 | tf_op jit(solution)/shard_map/convert.6
  2.0 0.4 fusion.8
  2.4 0.4 copy.39
  2.8 1.3 %collective-permute-start = (bf16[2,16,256]{2,1,0:T(8,128)(2,1)S(1)}, bf16[2,16,256]{2,1,0:T(8,128)(2,1)S(1)}, u32[]{:S(2)}, u32[]{:S(2)}) collective-permute-start(bf16[2,16,256]{2,1,0:T(8,128)(2,1)S(1)} %copy.39), channel_id=1, source_target_pairs={{8,0},{16,8},{24,16},{9,1},{17,9},{25,17},{10,2},{18,10},{26,18},{... | collective-permute-start | bytes 49160 | tf_op jit(solution)/shard_map/ppermute | solution.py:32
  4.1 0.4 copy.41
  4.5 4.6 %collective-permute-start.1 = (bf16[2,16,256]{2,1,0:T(8,128)(2,1)S(1)}, bf16[2,16,256]{2,1,0:T(8,128)(2,1)S(1)}, u32[]{:S(2)}, u32[]{:S(2)}) collective-permute-start(bf16[2,16,256]{2,1,0:T(8,128)(2,1)S(1)} %copy.41), channel_id=1, source_target_pairs={{0,8},{8,16},{16,24},{1,9},{9,17},{17,25},{2,10},{10,18},{18,26},{... | collective-permute-start | bytes 49160 | tf_op jit(solution)/shard_map/ppermute | solution.py:32
  9.1 0.0 copy-start.6
  9.1 0.0 copy-start.11
  9.1 0.1 pad_maximum_fusion.main_ref
  9.2 0.0 copy-start.12
  9.3 0.0 copy-start.14
  9.3 0.0 copy-start.8
  9.3 0.0 copy-start.7
  9.3 0.0 copy-start.15
  9.3 0.0 copy-start.5
  9.4 0.6 copy-done.6
  10.0 8.3 %all_gather.3 = bf16[160,1024]{1,0:T(8,128)(2,1)S(1)} all-gather(bf16[40,1024]{1,0:T(8,128)(2,1)S(1)} %copy-done.6), channel_id=1, replica_groups=mesh['gx'=4,'gy'=8] {'gx'}, dimensions={0}, use_global_device_ids=true | all-gather | bytes 409600 | tf_op jit(solution)/shard_map/all_gather | solution.py:314
  18.4 0.1 add_bitcast_fusion
  18.4 0.2 select_reduce_fusion
  18.7 0.1 add_select_fusion
  18.8 0.2 fusion.25
  19.0 0.6 fusion.42
  19.6 0.6 fusion.41
  20.2 0.0 copy-done.12
  20.3 0.0 copy-done.7
  20.3 0.0 copy-start.10
  20.5 0.0 copy-done.15
  20.5 0.2 copy.44
  20.7 0.1 fusion.16
  20.8 0.2 copy-done.10
  21.1 0.1 broadcast_add_fusion
  21.2 0.2 copy-done.9
  21.4 0.1 fusion.13.second_ref
  21.5 0.1 pad.127.clone
  21.6 0.0 collective-permute-done
  21.6 1.4 %copy.40 = bf16[2,16,256]{0,2,1:T(8,128)(2,1)} copy(bf16[2,16,256]{2,1,0:T(8,128)(2,1)S(1)} %collective-permute-done) | data formatting | bytes 32768 | tf_op jit(solution)/shard_map/ppermute | solution.py:32
  23.0 0.0 collective-permute-done.1
  23.0 1.4 %copy.42 = bf16[2,16,256]{0,2,1:T(8,128)(2,1)} copy(bf16[2,16,256]{2,1,0:T(8,128)(2,1)S(1)} %collective-permute-done.1) | data formatting | bytes 32768 | tf_op jit(solution)/shard_map/ppermute | solution.py:32
  24.4 2.2 %pad_maximum_fusion.1.side_ref = bf16[16,256,128]{2,1,0:T(8,128)(2,1)S(1)} fusion(bf16[16,256,2]{2,1,0:T(8,128)(2,1)} %bitcast.46, bf16[16,256,2]{2,1,0:T(8,128)(2,1)} %bitcast.45, bf16[128]{0:T(256)(128)(2,1)S(1)} %pad.127.clone), kind=kLoop, calls=%fused_computation.26 | loop fusion | flops 3145728 | bytes 1081600 | tf_op jit(solution)/shard_map/concatenate | solution.py:40
  26.6 0.6 pad_maximum_fusion.3
  27.2 6.8 %collective-permute-start.2 = (bf16[16,2,256]{2,1,0:T(2,128)(2,1)}, bf16[16,2,256]{2,1,0:T(2,128)(2,1)S(1)}, u32[]{:S(2)}, u32[]{:S(2)}) collective-permute-start(bf16[16,2,256]{2,1,0:T(2,128)(2,1)} %pad_maximum_fusion.3), channel_id=1, source_target_pairs={{0,1},{1,2},{2,3},{3,4},{4,5},{5,6},{6,7},{8,9},{9,10},{10,11},{11... | collective-permute-start | bytes 49160 | tf_op jit(solution)/shard_map/ppermute | solution.py:32
  34.0 0.6 pad_maximum_fusion.4
  34.6 1.9 %collective-permute-start.3 = (bf16[16,2,256]{2,1,0:T(2,128)(2,1)}, bf16[16,2,256]{2,1,0:T(2,128)(2,1)S(1)}, u32[]{:S(2)}, u32[]{:S(2)}) collective-permute-start(bf16[16,2,256]{2,1,0:T(2,128)(2,1)} %pad_maximum_fusion.4), channel_id=1, source_target_pairs={{1,0},{2,1},{3,2},{4,3},{5,4},{6,5},{7,6},{9,8},{10,9},{11,10},{12... | collective-permute-start | bytes 49160 | tf_op jit(solution)/shard_map/ppermute | solution.py:32
  36.5 0.5 and_select_fusion
  37.1 0.9 slice.71
  38.0 1.0 %copy.49 = f32[8,4,8,32]{2,3,0,1:T(8,128)} copy(f32[8,4,8,32]{3,2,1,0:T(8,128)S(1)} %slice.71) | data formatting | bytes 65536 | tf_op jit(solution)/shard_map/slice | solution.py:249
  39.0 5.0 %rev.7 = f32[4,256,8]{2,1,0:T(8,128)} reverse(f32[4,256,8]{2,1,0:T(8,128)} %bitcast.48), dimensions={2} | reverse | bytes 65536 | tf_op jit(solution)/shard_map/rev | solution.py:354
  44.1 0.8 slice.69
  44.9 1.0 %copy.48 = f32[8,4,8,32]{2,3,0,1:T(8,128)} copy(f32[8,4,8,32]{3,2,1,0:T(8,128)S(1)} %slice.69) | data formatting | bytes 65536 | tf_op jit(solution)/shard_map/slice | solution.py:249
  46.0 0.1 slice.67
  46.1 0.1 reshape.531
  46.2 0.8 slice.65
  47.1 0.1 reshape.530
  47.2 0.0 collective-permute-done.2.above_ref
  47.3 0.0 collective-permute-done.3.below_ref
  47.3 40.6 %shard_map.136 = f32[128,8,128]{2,1,0:T(8,128)S(1)} custom-call(bf16[16,256,128]{2,1,0:T(8,128)(2,1)S(1)} %pad_maximum_fusion.main_ref, bf16[16,256,128]{2,1,0:T(8,128)(2,1)S(1)} %pad_maximum_fusion.1.side_ref, bf16[16,2,256]{2,1,0:T(2,128)(2,1)S(1)} %collective-permute-done.2.above_ref, bf16[16,2,256]{2,1,0:T(2,128)(2,1)S(1)} %collective-permute-done.3.below_ref, ...), custom_call_target="tpu_custom_call" | custom-call | flops 20000000000 | bytes 8000000 | tf_op jit(solution)/shard_map/pallas_call | solution.py:203
  87.8 0.0 copy-start.4
  87.9 0.3 copy.45
  88.2 0.7 copy-done.1
  88.9 0.2 copy-done.2
  89.0 0.1 copy-done.3
  89.1 0.1 copy-done.4
  89.2 0.0 copy-done.13
  89.2 1.1 %add_convert_fusion = bf16[4,256,128]{2,1,0:T(8,128)(2,1)} fusion(f32[4,256,8]{2,1,0:T(8,128)S(1)} %copy-done.2, f32[4,256,8]{2,1,0:T(8,128)S(1)} %bitcast.49, f32[4,8,128]{2,1,0:T(8,128)S(1)} %rev.6, f32[4,8,128]{2,1,0:T(8,128)S(1)} %reshape.530, f32[4,256,128]{2,1,0:T(8,128)S(1)} %bitcast.51, bf16[4,256,128]{2,1,0:T(8,128)(2,1)S(1)} %copy-done.3, ...), kind=kLoop, calls=%fused_computation.33 | loop fusion | flops 2490368 | bytes 1543180 | tf_op jit(solution)/shard_map/convert_element_type | solution.py:367
  (47 shorter events, 0.5 us)
Async XLA Ops:
  0.0 2.0 %copy-start = (bf16[12,256,128]{2,1,0:T(8,128)(2,1)S(1)}, bf16[12,256,128]{2,1,0:T(8,128)(2,1)}, u32[]{:S(2)}) copy-start(bf16[12,256,128]{2,1,0:T(8,128)(2,1)} %param.16) | copy-start | bytes 2359300
  2.8 18.8 %collective-permute-start = (bf16[2,16,256]{2,1,0:T(8,128)(2,1)S(1)}, bf16[2,16,256]{2,1,0:T(8,128)(2,1)S(1)}, u32[]{:S(2)}, u32[]{:S(2)}) collective-permute-start(bf16[2,16,256]{2,1,0:T(8,128)(2,1)S(1)} %copy.39), channel_id=1, source_target_pairs={{8,0},{16,8},{24,16},{9,1},{17,9},{25,17},{10,2},{18,10},{26,18},{... | collective-permute-start | bytes 49160 | tf_op jit(solution)/shard_map/ppermute | solution.py:32
  4.5 18.5 %collective-permute-start.1 = (bf16[2,16,256]{2,1,0:T(8,128)(2,1)S(1)}, bf16[2,16,256]{2,1,0:T(8,128)(2,1)S(1)}, u32[]{:S(2)}, u32[]{:S(2)}) collective-permute-start(bf16[2,16,256]{2,1,0:T(8,128)(2,1)S(1)} %copy.41), channel_id=1, source_target_pairs={{0,8},{8,16},{16,24},{1,9},{9,17},{17,25},{2,10},{10,18},{18,26},{... | collective-permute-start | bytes 49160 | tf_op jit(solution)/shard_map/ppermute | solution.py:32
  9.1 0.9 copy-start.6
  9.1 9.3 %copy-start.11 = (s32[160]{0:T(256)S(1)}, s32[160]{0:T(256)}, u32[]{:S(2)}) copy-start(s32[160]{0:T(256)} %param.26) | copy-start | bytes 1924
  9.2 11.0 %copy-start.12 = (f32[256]{0:T(256)S(1)}, f32[256]{0:T(256)}, u32[]{:S(2)}) copy-start(f32[256]{0:T(256)} %param.20) | copy-start | bytes 3076
  9.3 11.0 %copy-start.14 = (f32[128]{0:T(128)S(1)}, f32[128]{0:T(128)}, u32[]{:S(2)}) copy-start(f32[128]{0:T(128)} %param.18) | copy-start | bytes 1540
  9.3 11.0 %copy-start.8 = (bf16[256,12]{0,1:T(8,128)(2,1)S(1)}, bf16[256,12]{0,1:T(8,128)(2,1)}, u32[]{:S(2)}) copy-start(bf16[256,12]{0,1:T(8,128)(2,1)} %param.19) | copy-start | bytes 18436
  9.3 11.0 %copy-start.7 = (bf16[3,3,128,16]{2,3,1,0:T(8,128)(2,1)S(1)}, bf16[3,3,128,16]{2,3,1,0:T(8,128)(2,1)}, u32[]{:S(2)}) copy-start(bf16[3,3,128,16]{2,3,1,0:T(8,128)(2,1)} %param.17) | copy-start | bytes 110596
  9.3 11.2 %copy-start.15 = (f32[128]{0:T(128)S(1)}, f32[128]{0:T(128)}, u32[]{:S(2)}) copy-start(f32[128]{0:T(128)} %param.22) | copy-start | bytes 1540
  9.3 11.2 %copy-start.5 = (bf16[3,3,128,128]{3,2,1,0:T(8,128)(2,1)S(1)}, bf16[3,3,128,128]{3,2,1,0:T(8,128)(2,1)}, u32[]{:S(2)}) copy-start(bf16[3,3,128,128]{3,2,1,0:T(8,128)(2,1)} %param.21) | copy-start | bytes 884740
  20.3 0.7 copy-start.10
  20.7 0.7 copy-start.9
  27.2 20.0 %collective-permute-start.2 = (bf16[16,2,256]{2,1,0:T(2,128)(2,1)}, bf16[16,2,256]{2,1,0:T(2,128)(2,1)S(1)}, u32[]{:S(2)}, u32[]{:S(2)}) collective-permute-start(bf16[16,2,256]{2,1,0:T(2,128)(2,1)} %pad_maximum_fusion.3), channel_id=1, source_target_pairs={{0,1},{1,2},{2,3},{3,4},{4,5},{5,6},{6,7},{8,9},{9,10},{10,11},{11... | collective-permute-start | bytes 49160 | tf_op jit(solution)/shard_map/ppermute | solution.py:32
  34.6 12.7 %collective-permute-start.3 = (bf16[16,2,256]{2,1,0:T(2,128)(2,1)}, bf16[16,2,256]{2,1,0:T(2,128)(2,1)S(1)}, u32[]{:S(2)}, u32[]{:S(2)}) collective-permute-start(bf16[16,2,256]{2,1,0:T(2,128)(2,1)} %pad_maximum_fusion.4), channel_id=1, source_target_pairs={{1,0},{2,1},{3,2},{4,3},{5,4},{6,5},{7,6},{9,8},{10,9},{11,10},{12... | collective-permute-start | bytes 49160 | tf_op jit(solution)/shard_map/ppermute | solution.py:32
  87.8 1.1 %copy-start.1 = (f32[8,4,8,32]{2,3,0,1:T(8,128)S(1)}, f32[8,4,8,32]{2,3,0,1:T(8,128)}, u32[]{:S(2)}) copy-start(f32[8,4,8,32]{2,3,0,1:T(8,128)} %copy.48) | copy-start | bytes 98308
  87.8 1.2 %copy-start.2 = (f32[4,256,8]{2,1,0:T(8,128)S(1)}, f32[4,256,8]{2,1,0:T(8,128)}, u32[]{:S(2)}) copy-start(f32[4,256,8]{2,1,0:T(8,128)} %rev.7) | copy-start | bytes 98308
  87.8 1.3 %copy-start.3 = (bf16[4,256,128]{2,1,0:T(8,128)(2,1)S(1)}, bf16[4,256,128]{2,1,0:T(8,128)(2,1)}, u32[]{:S(2)}) copy-start(bf16[4,256,128]{2,1,0:T(8,128)(2,1)} %param.15) | copy-start | bytes 786436
  87.8 1.4 %copy-start.4 = (bf16[4,256,128]{2,1,0:T(8,128)(2,1)S(1)}, bf16[4,256,128]{2,1,0:T(8,128)(2,1)}, u32[]{:S(2)}) copy-start(bf16[4,256,128]{2,1,0:T(8,128)(2,1)} %param.14) | copy-start | bytes 786436
  87.9 1.3 %copy-start.13 = (f32[128]{0:T(128)S(1)}, f32[128]{0:T(128)}, u32[]{:S(2)}) copy-start(f32[128]{0:T(128)} %get-tuple-element.31) | copy-start | bytes 1540

commit v2 on v1

--- a/solution.py
+++ b/solution.py
@@ -243,11 +243,6 @@
     return jnp.where(
         (distance >= 0) & (distance < band), RELAX_GAIN * (band - distance) / band, 0.0
     )
-
-
-def side_values(table, first_seg, seg_total, length):
-    chosen = table[first_seg : first_seg + seg_total]
-    return chosen.transpose(1, 2, 0, 3).reshape(table.shape[1], table.shape[2], length)
 
 
 def boundary_ids(col_ids, row_ids, col_count, row_count, segs_wide, segs_tall, segment_rows):
@@ -316,11 +311,11 @@
         jnp.bfloat16
     )
     delivered = jnp.dot(chosen, shard_rows, preferred_element_type=jnp.float32)
-    table = delivered.reshape(slot_count, channels, BAND, SEG)
-    south_side = side_values(table, 0, segs_wide, tile_cols)
-    north_side = side_values(table, segs_wide, segs_wide, tile_cols)
-    west_side = side_values(table, 2 * segs_wide, segs_tall, tile_rows)
-    east_side = side_values(table, 2 * segs_wide + segs_tall, segs_tall, tile_rows)
+    table = delivered.astype(jnp.bfloat16).reshape(slot_count, channels * BAND, SEG)
+    table = table.transpose(1, 0, 2).reshape(channels, BAND, slot_count * SEG)
+    south_side, north_side = table[:, :, :tile_cols], table[:, :, tile_cols : 2 * tile_cols]
+    west_side = table[:, :, 2 * tile_cols : 2 * tile_cols + tile_rows]
+    east_side = table[:, :, 2 * tile_cols + tile_rows :]
     state_hat = noisy_state.astype(jnp.float32) + spread * fresh_noise.astype(jnp.float32)
     net_in = jnp.concatenate(
         [scale_in * state_hat, conditioning.astype(jnp.float32)], axis=0
@@ -346,20 +341,34 @@
     north_weight = relax_weight(total_rows - 1.0 - global_rows, BAND)
     west_weight = relax_weight(global_cols, BAND)
     east_weight = relax_weight(total_cols - 1.0 - global_cols, BAND)
-    rest_rows = tile_rows - BAND
-    rest_cols = tile_cols - BAND
-    south_full = jnp.pad(south_side, ((0, 0), (0, rest_rows), (0, 0)))
-    north_full = jnp.pad(north_side[:, ::-1, :], ((0, 0), (rest_rows, 0), (0, 0)))
-    west_full = jnp.pad(west_side.transpose(0, 2, 1), ((0, 0), (0, 0), (0, rest_cols)))
-    east_full = jnp.pad(east_side.transpose(0, 2, 1)[:, :, ::-1], ((0, 0), (0, 0), (rest_cols, 0)))
-    numerator = (
-        denoised
-        + south_weight[None, :, None] * south_full
-        + north_weight[None, :, None] * north_full
-    )
-    numerator = (
-        numerator + west_weight[None, None, :] * west_full + east_weight[None, None, :] * east_full
-    )
+    depths = jnp.arange(BAND, dtype=jnp.float32)[:, None]
+
+    def placed(weight, distance):
+        return jnp.where(distance[None, :] == depths, weight[None, :], 0.0).astype(jnp.bfloat16)
+
+    by_row = jnp.concatenate(
+        [
+            placed(south_weight, global_rows),
+            placed(north_weight, total_rows - 1.0 - global_rows),
+        ],
+        axis=0,
+    )
+    by_col = jnp.concatenate(
+        [
+            placed(west_weight, global_cols),
+            placed(east_weight, total_cols - 1.0 - global_cols),
+        ],
+        axis=0,
+    )
+    every = (channels, 2 * BAND)
+    along_rows = jnp.concatenate(
+        [jnp.broadcast_to(by_row, every + by_row.shape[1:]), west_side, east_side], axis=1
+    )
+    along_cols = jnp.concatenate(
+        [south_side, north_side, jnp.broadcast_to(by_col, every + by_col.shape[1:])], axis=1
+    )
+    targets = jnp.einsum("ckh,ckw->chw", along_rows, along_cols, preferred_element_type=jnp.float32)
+    numerator = denoised + targets
     denominator = (
         1.0 + south_weight[:, None] + north_weight[:, None] + (west_weight + east_weight)[None, :]
     )

time: 91.1 us -> 78.5 us (0.86)
  local copies, waits for them, and re-layouts: 17.6 us -> 6.54 us
  other arithmetic: 7.41 us -> 4.68 us
  matrix products: 0.21 us -> 1.27 us
    slice x10 -> x2, local copies, waits for them, and re-layouts: 6 us -> 0.01 us  [the longest x1 0.01 us: on_device(): west_side = table[:, :, 2 * tile_cols:2 * tile_cols + tile_rows]]
    rev x2 -> x0, local copies, waits for them, and re-layouts: 5.04 us -> none  [the longest x1 5.02 us: on_device(): east_side.transpose(0, 2, 1)[:, :, ::-1]]
    dot_general x0 -> x1, matrix products: none -> 1.07 us  [on_device(): jnp.einsum('ckh,ckw->chw', along_rows, along_cols, preferred_element_type...]
    convert_element_type x1 -> x6, other arithmetic: 1.08 us -> 0.05 us  [the longest x4 0.04 us: placed(): jnp.where(distance[None, :] == depths, weight[None, :], 0.0)]
    unnamed x37 -> x31, local copies, waits for them, and re-layouts: 2.4 us -> 2.11 us
  transfers between devices with their start and end apart: 4 -> 4, of which waited for: 0 -> 1; matrix products, arithmetic and copies ran while one was open for 17% -> 5% of each run, Pallas kernels for 0% -> 0%
where the time goes in v2:
time: 78.5 us; the launch traced here: 78.1 us
  Pallas kernels  40.4 us (51%)
  starting transfers between devices  14.6 us (19%)
  blocking collectives  8.35 us (11%)
  local copies, waits for them, and re-layouts  6.54 us (8%)
  other arithmetic  4.68 us (6%)
  between operations  1.65 us (2%)
  matrix products  1.27 us (2%)
    pallas_call x1, Pallas kernels, residual_block(): pl.pallas_call(functools.partial(block_kernel, pairs, group, cols, width)...  40.4 us
    ppermute x4, starting transfers between devices, shifted(): return lax.ppermute(block, axis, pairs)  14.6 us
    all_gather x1, blocking collectives, on_device(): shard_rows = lax.all_gather(strip_table, 'gx', axis=0, tiled=True)  8.35 us
    ppermute x2, local copies, waits for them, and re-layouts, shifted(): return lax.ppermute(block, axis, pairs)  2.79 us
    concatenate x1, other arithmetic, halos(): jnp.concatenate([right.transpose(1, 2, 0), gap, left.transpose(1, 2, 0)],...  2.19 us
    unnamed x31, local copies, waits for them, and re-layouts  2.11 us
  transfers between devices with their start and end apart: 4, of which 1 were waited for; matrix products, arithmetic and copies ran while one was open for 5% of the time, Pallas kernels for 0%

profile of v2, /device:TPU:1, one launch (start us, length us, event | category | flops | bytes accessed | tf_op | source)
XLA Modules:
  0.0 78.1 jit_solution(10105158758027075535)
XLA Ops:
  0.0 0.0 copy-start
  0.9 1.1 %multiply_convert_fusion = bf16[4,256,128]{2,1,0:T(8,128)(2,1)S(1)} fusion(bf16[4,256,128]{2,1,0:T(8,128)(2,1)} %param.15, bf16[4,256,128]{2,1,0:T(8,128)(2,1)} %param.14, f32[]{:T(128)S(6)} %div.41, f32[]{:T(128)S(6)} %mul_shard_map.6), kind=kLoop, calls=%fused_computation.40 | loop fusion | flops 786432 | bytes 786440 | tf_op jit(solution)/shard_map/convert.6
  2.0 0.0 copy-done
  2.0 0.4 fusion.13
  2.4 0.4 copy.30
  2.8 1.3 %collective-permute-start = (bf16[2,16,256]{2,1,0:T(8,128)(2,1)S(1)}, bf16[2,16,256]{2,1,0:T(8,128)(2,1)S(1)}, u32[]{:S(2)}, u32[]{:S(2)}) collective-permute-start(bf16[2,16,256]{2,1,0:T(8,128)(2,1)S(1)} %copy.30), channel_id=1, source_target_pairs={{8,0},{16,8},{24,16},{9,1},{17,9},{25,17},{10,2},{18,10},{26,18},{... | collective-permute-start | bytes 49160 | tf_op jit(solution)/shard_map/ppermute | solution.py:32
  4.1 0.4 copy.32
  4.5 4.6 %collective-permute-start.1 = (bf16[2,16,256]{2,1,0:T(8,128)(2,1)S(1)}, bf16[2,16,256]{2,1,0:T(8,128)(2,1)S(1)}, u32[]{:S(2)}, u32[]{:S(2)}) collective-permute-start(bf16[2,16,256]{2,1,0:T(8,128)(2,1)S(1)} %copy.32), channel_id=1, source_target_pairs={{0,8},{8,16},{16,24},{1,9},{9,17},{17,25},{2,10},{10,18},{18,26},{... | collective-permute-start | bytes 49160 | tf_op jit(solution)/shard_map/ppermute | solution.py:32
  9.1 0.0 copy-start.4
  9.1 0.0 copy-start.9
  9.1 0.1 pad_maximum_fusion.main_ref
  9.2 0.0 copy-start.10
  9.3 0.0 copy-start.11
  9.3 0.0 copy-start.6
  9.3 0.0 copy-start.5
  9.3 0.7 copy-done.4
  10.0 8.3 %all_gather.3 = bf16[160,1024]{1,0:T(8,128)(2,1)S(1)} all-gather(bf16[40,1024]{1,0:T(8,128)(2,1)S(1)} %copy-done.4), channel_id=1, replica_groups=mesh['gx'=4,'gy'=8] {'gx'}, dimensions={0}, use_global_device_ids=true | all-gather | bytes 409600 | tf_op jit(solution)/shard_map/all_gather | solution.py:309
  18.4 0.1 add_bitcast_fusion
  18.4 0.0 copy-done.9
  18.4 0.2 select_reduce_fusion
  18.7 0.1 add_select_fusion
  18.8 0.0 copy-start.12
  18.8 0.0 copy-start.1
  18.8 0.2 convolution_convert_fusion
  19.0 0.2 reshape.511
  19.2 0.1 copy.37
  19.2 0.1 reshape.512
  19.5 0.0 copy-done.10
  19.6 0.0 copy-done.11
  19.6 0.0 copy-done.6
  19.6 0.0 copy-done.5
  19.8 0.0 copy-done.12
  19.8 0.0 copy-done.1
  19.8 0.2 copy.35
  20.1 0.0 copy-start.7
  20.1 0.1 fusion.21
  20.2 0.0 copy-start.8
  20.3 0.1 broadcast_add_fusion
  20.4 0.4 copy-done.7
  20.8 0.1 fusion.18.second_ref
  20.8 0.1 copy-done.8
  20.9 0.1 pad.117.clone
  21.0 0.0 collective-permute-done
  21.0 1.4 %copy.31 = bf16[2,16,256]{0,2,1:T(8,128)(2,1)} copy(bf16[2,16,256]{2,1,0:T(8,128)(2,1)S(1)} %collective-permute-done) | data formatting | bytes 32768 | tf_op jit(solution)/shard_map/ppermute | solution.py:32
  22.4 0.0 collective-permute-done.1
  22.4 1.4 %copy.33 = bf16[2,16,256]{0,2,1:T(8,128)(2,1)} copy(bf16[2,16,256]{2,1,0:T(8,128)(2,1)S(1)} %collective-permute-done.1) | data formatting | bytes 32768 | tf_op jit(solution)/shard_map/ppermute | solution.py:32
  23.8 2.2 %pad_maximum_fusion.1.side_ref = bf16[16,256,128]{2,1,0:T(8,128)(2,1)S(1)} fusion(bf16[16,256,2]{2,1,0:T(8,128)(2,1)} %bitcast.31, bf16[16,256,2]{2,1,0:T(8,128)(2,1)} %bitcast.30, bf16[128]{0:T(256)(128)(2,1)S(1)} %pad.117.clone), kind=kLoop, calls=%fused_computation.33 | loop fusion | flops 3145728 | bytes 1081600 | tf_op jit(solution)/shard_map/concatenate | solution.py:40
  26.0 5.6 %collective-permute-start.3 = (bf16[16,2,256]{2,1,0:T(2,128)(2,1)S(1)}, bf16[16,2,256]{2,1,0:T(2,128)(2,1)S(1)}, u32[]{:S(2)}, u32[]{:S(2)}) collective-permute-start(bf16[16,2,256]{2,1,0:T(2,128)(2,1)S(1)} %pad_maximum_fusion.4), channel_id=1, source_target_pairs={{1,0},{2,1},{3,2},{4,3},{5,4},{6,5},{7,6},{9,8},{10,9},{11,10},{12... | collective-permute-start | bytes 49160 | tf_op jit(solution)/shard_map/ppermute | solution.py:32
  31.6 3.1 %collective-permute-start.2 = (bf16[16,2,256]{2,1,0:T(2,128)(2,1)S(1)}, bf16[16,2,256]{2,1,0:T(2,128)(2,1)S(1)}, u32[]{:S(2)}, u32[]{:S(2)}) collective-permute-start(bf16[16,2,256]{2,1,0:T(2,128)(2,1)S(1)} %pad_maximum_fusion.3), channel_id=1, source_target_pairs={{0,1},{1,2},{2,3},{3,4},{4,5},{5,6},{6,7},{8,9},{9,10},{10,11},{11... | collective-permute-start | bytes 49160 | tf_op jit(solution)/shard_map/ppermute | solution.py:32
  34.9 0.0 collective-permute-done.3.below_ref
  35.0 0.7 collective-permute-done.2.above_ref
  35.6 40.4 %shard_map.136 = f32[128,8,128]{2,1,0:T(8,128)S(1)} custom-call(bf16[16,256,128]{2,1,0:T(8,128)(2,1)S(1)} %pad_maximum_fusion.main_ref, bf16[16,256,128]{2,1,0:T(8,128)(2,1)S(1)} %pad_maximum_fusion.1.side_ref, bf16[16,2,256]{2,1,0:T(2,128)(2,1)S(1)} %collective-permute-done.2.above_ref, bf16[16,2,256]{2,1,0:T(2,128)(2,1)S(1)} %collective-permute-done.3.below_ref, ...), custom_call_target="tpu_custom_call" | custom-call | flops 20000000000 | bytes 8000000 | tf_op jit(solution)/shard_map/pallas_call | solution.py:203
  76.0 0.0 copy-start.2
  76.0 0.0 copy-start.3
  76.1 0.3 copy.36
  76.4 0.6 copy-done.2
  77.0 0.1 copy-done.3
  77.1 1.1 %fusion.11 = bf16[4,256,128]{2,1,0:T(8,128)(2,1)} fusion(f32[4,256,128]{2,1,0:T(8,128)S(1)} %bitcast.36, bf16[4,256,128]{2,1,0:T(8,128)(2,1)S(1)} %copy-done.2, bf16[4,256,128]{2,1,0:T(8,128)(2,1)S(1)} %copy-done.3, f32[256,128]{1,0:T(8,128)S(1)} %broadcast_add_fusion, f32[]{:T(128)S(6)} %div.39, f32[]{:T(128)S(6)} %div.38, f32[]{:T(128)S(6)} %mul_shard_map.6, ...), kind=kOutput, calls=%fused_computation.23 | convolution fusion | flops 10256384 | bytes 1540108 | tf_op jit(solution)/shard_map/ckh,ckw->chw/dot_general | solution.py:370
  (48 shorter events, 0.5 us)
Async XLA Ops:
  0.0 2.0 %copy-start = (bf16[12,256,128]{2,1,0:T(8,128)(2,1)S(1)}, bf16[12,256,128]{2,1,0:T(8,128)(2,1)}, u32[]{:S(2)}) copy-start(bf16[12,256,128]{2,1,0:T(8,128)(2,1)} %param.16) | copy-start | bytes 2359300
  2.8 18.1 %collective-permute-start = (bf16[2,16,256]{2,1,0:T(8,128)(2,1)S(1)}, bf16[2,16,256]{2,1,0:T(8,128)(2,1)S(1)}, u32[]{:S(2)}, u32[]{:S(2)}) collective-permute-start(bf16[2,16,256]{2,1,0:T(8,128)(2,1)S(1)} %copy.30), channel_id=1, source_target_pairs={{8,0},{16,8},{24,16},{9,1},{17,9},{25,17},{10,2},{18,10},{26,18},{... | collective-permute-start | bytes 49160 | tf_op jit(solution)/shard_map/ppermute | solution.py:32
  4.5 17.9 %collective-permute-start.1 = (bf16[2,16,256]{2,1,0:T(8,128)(2,1)S(1)}, bf16[2,16,256]{2,1,0:T(8,128)(2,1)S(1)}, u32[]{:S(2)}, u32[]{:S(2)}) collective-permute-start(bf16[2,16,256]{2,1,0:T(8,128)(2,1)S(1)} %copy.32), channel_id=1, source_target_pairs={{0,8},{8,16},{16,24},{1,9},{9,17},{17,25},{2,10},{10,18},{18,26},{... | collective-permute-start | bytes 49160 | tf_op jit(solution)/shard_map/ppermute | solution.py:32
  9.1 0.9 %copy-start.4 = (bf16[40,1024]{1,0:T(8,128)(2,1)S(1)}, bf16[40,1024]{1,0:T(8,128)(2,1)}, u32[]{:S(2)}) copy-start(bf16[40,1024]{1,0:T(8,128)(2,1)} %param.25) | copy-start | bytes 245764
  9.1 9.3 %copy-start.9 = (s32[160]{0:T(256)S(1)}, s32[160]{0:T(256)}, u32[]{:S(2)}) copy-start(s32[160]{0:T(256)} %param.26) | copy-start | bytes 1924
  9.2 10.3 %copy-start.10 = (f32[256]{0:T(256)S(1)}, f32[256]{0:T(256)}, u32[]{:S(2)}) copy-start(f32[256]{0:T(256)} %param.20) | copy-start | bytes 3076
  9.3 10.3 %copy-start.11 = (f32[128]{0:T(128)S(1)}, f32[128]{0:T(128)}, u32[]{:S(2)}) copy-start(f32[128]{0:T(128)} %param.18) | copy-start | bytes 1540
  9.3 10.4 %copy-start.6 = (bf16[256,12]{0,1:T(8,128)(2,1)S(1)}, bf16[256,12]{0,1:T(8,128)(2,1)}, u32[]{:S(2)}) copy-start(bf16[256,12]{0,1:T(8,128)(2,1)} %param.19) | copy-start | bytes 18436
  9.3 10.4 %copy-start.5 = (bf16[3,3,128,16]{2,3,1,0:T(8,128)(2,1)S(1)}, bf16[3,3,128,16]{2,3,1,0:T(8,128)(2,1)}, u32[]{:S(2)}) copy-start(bf16[3,3,128,16]{2,3,1,0:T(8,128)(2,1)} %param.17) | copy-start | bytes 110596
  18.8 1.1 %copy-start.12 = (f32[128]{0:T(128)S(1)}, f32[128]{0:T(128)}, u32[]{:S(2)}) copy-start(f32[128]{0:T(128)} %param.22) | copy-start | bytes 1540
  18.8 1.1 %copy-start.1 = (bf16[3,3,128,128]{3,2,1,0:T(8,128)(2,1)S(1)}, bf16[3,3,128,128]{3,2,1,0:T(8,128)(2,1)}, u32[]{:S(2)}) copy-start(bf16[3,3,128,128]{3,2,1,0:T(8,128)(2,1)} %param.21) | copy-start | bytes 884740
  20.1 0.7 copy-start.7
  20.2 0.7 copy-start.8
  26.0 8.9 %collective-permute-start.3 = (bf16[16,2,256]{2,1,0:T(2,128)(2,1)S(1)}, bf16[16,2,256]{2,1,0:T(2,128)(2,1)S(1)}, u32[]{:S(2)}, u32[]{:S(2)}) collective-permute-start(bf16[16,2,256]{2,1,0:T(2,128)(2,1)S(1)} %pad_maximum_fusion.4), channel_id=1, source_target_pairs={{1,0},{2,1},{3,2},{4,3},{5,4},{6,5},{7,6},{9,8},{10,9},{11,10},{12... | collective-permute-start | bytes 49160 | tf_op jit(solution)/shard_map/ppermute | solution.py:32
  31.6 4.0 %collective-permute-start.2 = (bf16[16,2,256]{2,1,0:T(2,128)(2,1)S(1)}, bf16[16,2,256]{2,1,0:T(2,128)(2,1)S(1)}, u32[]{:S(2)}, u32[]{:S(2)}) collective-permute-start(bf16[16,2,256]{2,1,0:T(2,128)(2,1)S(1)} %pad_maximum_fusion.3), channel_id=1, source_target_pairs={{0,1},{1,2},{2,3},{3,4},{4,5},{5,6},{6,7},{8,9},{9,10},{10,11},{11... | collective-permute-start | bytes 49160 | tf_op jit(solution)/shard_map/ppermute | solution.py:32
  76.0 1.0 %copy-start.2 = (bf16[4,256,128]{2,1,0:T(8,128)(2,1)S(1)}, bf16[4,256,128]{2,1,0:T(8,128)(2,1)}, u32[]{:S(2)}) copy-start(bf16[4,256,128]{2,1,0:T(8,128)(2,1)} %param.15) | copy-start | bytes 786436
  76.0 1.0 %copy-start.3 = (bf16[4,256,128]{2,1,0:T(8,128)(2,1)S(1)}, bf16[4,256,128]{2,1,0:T(8,128)(2,1)}, u32[]{:S(2)}) copy-start(bf16[4,256,128]{2,1,0:T(8,128)(2,1)} %param.14) | copy-start | bytes 786436

commit v3 on v2

--- a/solution.py
+++ b/solution.py
@@ -19,7 +19,7 @@
 NOISE_GAIN = 1.007
 SIGMA_DATA = 0.5
 RELAX_GAIN = 3.0
-SUB = 4
+SUB = 1
 ROOT_HALF = 0.7071067811865476
 
 
@@ -36,11 +36,13 @@
     channels, rows, cols = net_in.shape
     left = shifted(net_in[:, :, cols - 2 :].transpose(2, 0, 1), "gx", 1)
     right = shifted(net_in[:, :, :2].transpose(2, 0, 1), "gx", -1)
-    gap = jnp.zeros((channels, rows, cols - 4), net_in.dtype)
-    beside = jnp.concatenate([right.transpose(1, 2, 0), gap, left.transpose(1, 2, 0)], axis=2)
-    tail = jnp.concatenate([net_in[:, rows - 2 :], beside[:, rows - 2 :]], axis=2)
-    head = jnp.concatenate([net_in[:, :2], beside[:, :2]], axis=2)
-    return beside, shifted(tail, "gy", 1), shifted(head, "gy", -1)
+    gap = jnp.zeros((channels, 2, cols - 4), net_in.dtype)
+
+    def whole(top):
+        ends = [side[:, :, top : top + 2].transpose(1, 2, 0) for side in (right, left)]
+        return jnp.concatenate([net_in[:, top : top + 2], ends[0], gap, ends[1]], axis=2)
+
+    return left, right, shifted(whole(rows - 2), "gy", 1), shifted(whole(0), "gy", -1)
 
 
 def three_parts(values):
@@ -99,16 +101,20 @@
     )
 
 
-def block_kernel(pairs, group, cols, width, main_ref, side_ref, above_ref, below_ref, first_ref,
-                 second_ref, out_ref, proj_ref, net_ref, edge_ref, held, patches):
+def block_kernel(pairs, group, cols, width, main_ref, left_ref, right_ref, above_ref, below_ref,
+                 first_ref, second_ref, out_ref, proj_ref, net_ref, edge_ref, held, patches):
     tile_col, tile_row = lax.axis_index("gx"), lax.axis_index("gy")
     last_col, last_row = lax.axis_size("gx") - 1, lax.axis_size("gy") - 1
     wide = cols + 16
     inner, rows = main_ref.shape[0], main_ref.shape[1]
+    gap = jnp.zeros((cols - 4, rows), jnp.float32)
     for c in range(inner):
         spot = pl.ds(2 * inner + c, rows, stride=inner)
         net_ref[spot] = main_ref[c].astype(jnp.float32)
-        edge_ref[spot] = side_ref[c].astype(jnp.float32)
+        beside = jnp.concatenate(
+            [right_ref[:, c].astype(jnp.float32), gap, left_ref[:, c].astype(jnp.float32)], axis=0
+        )
+        edge_ref[spot] = beside.T
         upper, lower = above_ref[c].astype(jnp.float32), below_ref[c].astype(jnp.float32)
         for r in range(2):
             at, end = r * inner + c, (rows + 2 + r) * inner + c
@@ -193,7 +199,7 @@
         held[0, :, :depth] = held[group, :, :depth]
 
 
-def residual_block(net_in, beside, above, below, first_w, second_w, skip_w, out_w):
+def residual_block(net_in, left, right, above, below, first_w, second_w, skip_w, out_w):
     inner, rows, cols = net_in.shape
     pairs = rows // 2
     width = second_w.shape[1] // 2
@@ -203,7 +209,7 @@
     return pl.pallas_call(
         functools.partial(block_kernel, pairs, group, cols, width),
         out_shape=jax.ShapeDtypeStruct((pairs, out_w.shape[0], cols), jnp.float32),
-        in_specs=[pl.BlockSpec(memory_space=pltpu.VMEM)] * 7,
+        in_specs=[pl.BlockSpec(memory_space=pltpu.VMEM)] * 8,
         out_specs=pl.BlockSpec(memory_space=pltpu.VMEM),
         scratch_shapes=[
             pltpu.VMEM(((rows + 4) * inner, cols), jnp.float32),
@@ -213,7 +219,7 @@
         ],
         compiler_params=pltpu.CompilerParams(vmem_limit_bytes=48 * 1024 * 1024),
         cost_estimate=pl.CostEstimate(flops=20_000_000_000, bytes_accessed=8_000_000, transcendentals=4_500_000),
-    )(net_in, beside, above, below, first_w, second_w, out_w)
+    )(net_in, left, right, above, below, first_w, second_w, out_w)
 
 
 def noise_levels(step_index, total_steps):

time: 78.5 us -> 75.9 us (0.967)
  waiting for transfers between devices: 0.66 us -> 2.94 us
  other arithmetic: 4.68 us -> 2.55 us
  local copies, waits for them, and re-layouts: 6.54 us -> 4.71 us
  Pallas kernels: 40.4 us -> 39.5 us
    ppermute x2 -> x0, local copies, waits for them, and re-layouts: 2.79 us -> none  [shifted(): return lax.ppermute(block, axis, pairs)]
    ppermute x4, waiting for transfers between devices: 0.66 us -> 2.94 us  [shifted(): return lax.ppermute(block, axis, pairs)]
    concatenate x3 -> x1, other arithmetic: 2.22 us -> 0.1 us  [whole(): jnp.concatenate([net_in[:, top:top + 2], ends[0], gap, ends[1]], axis=2)]
    pallas_call x1, Pallas kernels: 40.4 us -> 39.5 us  [residual_block(): pl.pallas_call(functools.partial(block_kernel, pairs, group, cols, width)...]
    unnamed x31 -> x35, local copies, waits for them, and re-layouts: 2.11 us -> 2.95 us
  transfers between devices with their start and end apart: 4 -> 4, of which waited for: 1 -> 1; matrix products, arithmetic and copies ran while one was open for 5% -> 3% of each run, Pallas kernels for 0% -> 0%
where the time goes in v3:
time: 75.9 us; the launch traced here: 75.6 us
  Pallas kernels  39.5 us (52%)
  starting transfers between devices  14.6 us (19%)
  blocking collectives  8.35 us (11%)
  local copies, waits for them, and re-layouts  4.71 us (6%)
  waiting for transfers between devices  2.94 us (4%)
  other arithmetic  2.55 us (3%)
  between operations  1.63 us (2%)
  matrix products  1.27 us (2%)
    pallas_call x1, Pallas kernels, residual_block(): pl.pallas_call(functools.partial(block_kernel, pairs, group, cols, width)...  39.5 us
    ppermute x4, starting transfers between devices, shifted(): return lax.ppermute(block, axis, pairs)  14.6 us
    all_gather x1, blocking collectives, on_device(): shard_rows = lax.all_gather(strip_table, 'gx', axis=0, tiled=True)  8.35 us
    unnamed x35, local copies, waits for them, and re-layouts  2.95 us
    ppermute x4, waiting for transfers between devices, shifted(): return lax.ppermute(block, axis, pairs)  2.94 us
  transfers between devices with their start and end apart: 4, of which 1 were waited for; matrix products, arithmetic and copies ran while one was open for 3% of the time, Pallas kernels for 0%

profile of v3, /device:TPU:1, one launch (start us, length us, event | category | flops | bytes accessed | tf_op | source)
XLA Modules:
  0.0 75.6 jit_solution(18063700823031661303)
XLA Ops:
  0.0 0.0 copy-start
  0.9 1.1 %multiply_convert_fusion = bf16[4,256,128]{2,1,0:T(8,128)(2,1)S(1)} fusion(bf16[4,256,128]{2,1,0:T(8,128)(2,1)} %param.15, bf16[4,256,128]{2,1,0:T(8,128)(2,1)} %param.14, f32[]{:T(128)S(6)} %div.41, f32[]{:T(128)S(6)} %mul_shard_map.6), kind=kLoop, calls=%fused_computation.39 | loop fusion | flops 786432 | bytes 786440 | tf_op jit(solution)/shard_map/convert.6
  2.0 0.0 copy-done
  2.0 0.4 fusion.15
  2.4 0.4 copy.37
  2.8 1.3 %collective-permute-start.1 = (bf16[2,16,256]{2,1,0:T(8,128)(2,1)S(1)}, bf16[2,16,256]{2,1,0:T(8,128)(2,1)S(1)}, u32[]{:S(2)}, u32[]{:S(2)}) collective-permute-start(bf16[2,16,256]{2,1,0:T(8,128)(2,1)S(1)} %copy.37), channel_id=1, source_target_pairs={{8,0},{16,8},{24,16},{9,1},{17,9},{25,17},{10,2},{18,10},{26,18},{... | collective-permute-start | bytes 49160 | tf_op jit(solution)/shard_map/ppermute | solution.py:32
  4.1 0.4 copy.36
  4.5 4.6 %collective-permute-start = (bf16[2,16,256]{2,1,0:T(8,128)(2,1)S(1)}, bf16[2,16,256]{2,1,0:T(8,128)(2,1)S(1)}, u32[]{:S(2)}, u32[]{:S(2)}) collective-permute-start(bf16[2,16,256]{2,1,0:T(8,128)(2,1)S(1)} %copy.36), channel_id=1, source_target_pairs={{0,8},{8,16},{16,24},{1,9},{9,17},{17,25},{2,10},{10,18},{18,26},{... | collective-permute-start | bytes 49160 | tf_op jit(solution)/shard_map/ppermute | solution.py:32
  9.1 0.0 copy-start.4
  9.1 0.0 copy-start.9
  9.1 0.1 pad_maximum_fusion.main_ref
  9.2 0.0 copy-start.10
  9.3 0.0 copy-start.11
  9.3 0.0 copy-start.6
  9.3 0.0 copy-start.5
  9.3 0.7 copy-done.4
  10.0 8.3 %all_gather.3 = bf16[160,1024]{1,0:T(8,128)(2,1)S(1)} all-gather(bf16[40,1024]{1,0:T(8,128)(2,1)S(1)} %copy-done.4), channel_id=1, replica_groups=mesh['gx'=4,'gy'=8] {'gx'}, dimensions={0}, use_global_device_ids=true | all-gather | bytes 409600 | tf_op jit(solution)/shard_map/all_gather | solution.py:315
  18.4 0.1 add_bitcast_fusion
  18.4 0.0 copy-done.9
  18.4 0.2 select_reduce_fusion
  18.7 0.1 add_select_fusion
  18.8 0.0 copy-start.12
  18.8 0.0 copy-start.1
  18.8 0.2 convolution_convert_fusion
  19.0 0.2 reshape.511
  19.2 0.1 copy.45
  19.2 0.1 reshape.512
  19.5 0.0 copy-done.10
  19.6 0.0 copy-done.11
  19.6 0.0 copy-done.6
  19.6 0.0 copy-done.5
  19.8 0.0 copy-done.12
  19.8 0.0 copy-done.1
  19.8 0.2 copy.43
  20.1 0.0 copy-start.7
  20.1 0.1 fusion.21
  20.2 0.0 copy-start.8
  20.3 0.1 broadcast_add_fusion
  20.4 0.4 copy-done.7
  20.8 0.1 fusion.18.second_ref
  20.8 0.1 copy-done.8
  20.9 0.1 pad.118.clone
  21.0 0.0 collective-permute-done.1.right_ref
  21.0 0.1 fusion.58
  21.0 0.2 copy.46
  21.3 0.0 collective-permute-done.left_ref
  21.3 0.1 fusion.59
  21.3 0.2 copy.47
  21.5 0.2 copy.48
  21.8 0.2 copy.49
  22.0 0.1 pad_maximum_fusion.3
  22.1 6.8 %collective-permute-start.2 = (bf16[16,2,256]{2,1,0:T(2,128)(2,1)S(1)}, bf16[16,2,256]{2,1,0:T(2,128)(2,1)S(1)}, u32[]{:S(2)}, u32[]{:S(2)}) collective-permute-start(bf16[16,2,256]{2,1,0:T(2,128)(2,1)S(1)} %get-tuple-element.29), channel_id=1, source_target_pairs={{0,1},{1,2},{2,3},{3,4},{4,5},{5,6},{6,7},{8,9},{9,10},{10,11},{11... | collective-permute-start | bytes 49160 | tf_op jit(solution)/shard_map/ppermute | solution.py:32
  28.9 1.9 %collective-permute-start.3 = (bf16[16,2,256]{2,1,0:T(2,128)(2,1)S(1)}, bf16[16,2,256]{2,1,0:T(2,128)(2,1)S(1)}, u32[]{:S(2)}, u32[]{:S(2)}) collective-permute-start(bf16[16,2,256]{2,1,0:T(2,128)(2,1)S(1)} %get-tuple-element.28), channel_id=1, source_target_pairs={{1,0},{2,1},{3,2},{4,3},{5,4},{6,5},{7,6},{9,8},{10,9},{11,10},{12... | collective-permute-start | bytes 49160 | tf_op jit(solution)/shard_map/ppermute | solution.py:32
  31.0 0.0 collective-permute-done.2.above_ref
  31.0 2.9 %collective-permute-done.3.below_ref = bf16[16,2,256]{2,1,0:T(2,128)(2,1)S(1)} collective-permute-done((bf16[16,2,256]{2,1,0:T(2,128)(2,1)S(1)}, bf16[16,2,256]{2,1,0:T(2,128)(2,1)S(1)}, u32[]{:S(2)}, u32[]{:S(2)}) %collective-permute-start.3) | collective-permute-done | bytes 16416 | tf_op jit(solution)/shard_map/ppermute | solution.py:32
  33.9 39.5 %shard_map.136 = f32[128,8,128]{2,1,0:T(8,128)S(1)} custom-call(bf16[16,256,128]{2,1,0:T(8,128)(2,1)S(1)} %pad_maximum_fusion.main_ref, bf16[2,16,256]{2,1,0:T(8,128)(2,1)S(1)} %collective-permute-done.left_ref, bf16[2,16,256]{2,1,0:T(8,128)(2,1)S(1)} %collective-permute-done.1.right_ref, bf16[16,2,256]{2,1,0:T(2,128)(2,1)S(1)} %collective-permute-done.2.above_ref, ...), custom_call_target="tpu_custom_call" | custom-call | flops 20000000000 | bytes 8000000 | tf_op jit(solution)/shard_map/pallas_call | solution.py:209
  73.5 0.0 copy-start.2
  73.5 0.0 copy-start.3
  73.5 0.3 copy.44
  73.8 0.6 copy-done.2
  74.4 0.1 copy-done.3
  74.5 1.1 %fusion.11 = bf16[4,256,128]{2,1,0:T(8,128)(2,1)} fusion(f32[4,256,128]{2,1,0:T(8,128)S(1)} %bitcast.36, bf16[4,256,128]{2,1,0:T(8,128)(2,1)S(1)} %copy-done.2, bf16[4,256,128]{2,1,0:T(8,128)(2,1)S(1)} %copy-done.3, f32[256,128]{1,0:T(8,128)S(1)} %broadcast_add_fusion, f32[]{:T(128)S(6)} %div.39, f32[]{:T(128)S(6)} %div.38, f32[]{:T(128)S(6)} %mul_shard_map.6, ...), kind=kOutput, calls=%fused_computation.23 | convolution fusion | flops 10256384 | bytes 1540108 | tf_op jit(solution)/shard_map/ckh,ckw->chw/dot_general | solution.py:376
  (45 shorter events, 0.4 us)
Async XLA Ops:
  0.0 2.0 %copy-start = (bf16[12,256,128]{2,1,0:T(8,128)(2,1)S(1)}, bf16[12,256,128]{2,1,0:T(8,128)(2,1)}, u32[]{:S(2)}) copy-start(bf16[12,256,128]{2,1,0:T(8,128)(2,1)} %param.16) | copy-start | bytes 2359300
  2.8 18.1 %collective-permute-start.1 = (bf16[2,16,256]{2,1,0:T(8,128)(2,1)S(1)}, bf16[2,16,256]{2,1,0:T(8,128)(2,1)S(1)}, u32[]{:S(2)}, u32[]{:S(2)}) collective-permute-start(bf16[2,16,256]{2,1,0:T(8,128)(2,1)S(1)} %copy.37), channel_id=1, source_target_pairs={{8,0},{16,8},{24,16},{9,1},{17,9},{25,17},{10,2},{18,10},{26,18},{... | collective-permute-start | bytes 49160 | tf_op jit(solution)/shard_map/ppermute | solution.py:32
  4.5 16.8 %collective-permute-start = (bf16[2,16,256]{2,1,0:T(8,128)(2,1)S(1)}, bf16[2,16,256]{2,1,0:T(8,128)(2,1)S(1)}, u32[]{:S(2)}, u32[]{:S(2)}) collective-permute-start(bf16[2,16,256]{2,1,0:T(8,128)(2,1)S(1)} %copy.36), channel_id=1, source_target_pairs={{0,8},{8,16},{16,24},{1,9},{9,17},{17,25},{2,10},{10,18},{18,26},{... | collective-permute-start | bytes 49160 | tf_op jit(solution)/shard_map/ppermute | solution.py:32
  9.1 0.9 %copy-start.4 = (bf16[40,1024]{1,0:T(8,128)(2,1)S(1)}, bf16[40,1024]{1,0:T(8,128)(2,1)}, u32[]{:S(2)}) copy-start(bf16[40,1024]{1,0:T(8,128)(2,1)} %param.25) | copy-start | bytes 245764
  9.1 9.3 %copy-start.9 = (s32[160]{0:T(256)S(1)}, s32[160]{0:T(256)}, u32[]{:S(2)}) copy-start(s32[160]{0:T(256)} %param.26) | copy-start | bytes 1924
  9.2 10.3 %copy-start.10 = (f32[256]{0:T(256)S(1)}, f32[256]{0:T(256)}, u32[]{:S(2)}) copy-start(f32[256]{0:T(256)} %param.20) | copy-start | bytes 3076
  9.3 10.3 %copy-start.11 = (f32[128]{0:T(128)S(1)}, f32[128]{0:T(128)}, u32[]{:S(2)}) copy-start(f32[128]{0:T(128)} %param.18) | copy-start | bytes 1540
  9.3 10.4 %copy-start.6 = (bf16[256,12]{0,1:T(8,128)(2,1)S(1)}, bf16[256,12]{0,1:T(8,128)(2,1)}, u32[]{:S(2)}) copy-start(bf16[256,12]{0,1:T(8,128)(2,1)} %param.19) | copy-start | bytes 18436
  9.3 10.4 %copy-start.5 = (bf16[3,3,128,16]{2,3,1,0:T(8,128)(2,1)S(1)}, bf16[3,3,128,16]{2,3,1,0:T(8,128)(2,1)}, u32[]{:S(2)}) copy-start(bf16[3,3,128,16]{2,3,1,0:T(8,128)(2,1)} %param.17) | copy-start | bytes 110596
  18.8 1.1 %copy-start.12 = (f32[128]{0:T(128)S(1)}, f32[128]{0:T(128)}, u32[]{:S(2)}) copy-start(f32[128]{0:T(128)} %param.22) | copy-start | bytes 1540
  18.8 1.1 %copy-start.1 = (bf16[3,3,128,128]{3,2,1,0:T(8,128)(2,1)S(1)}, bf16[3,3,128,128]{3,2,1,0:T(8,128)(2,1)}, u32[]{:S(2)}) copy-start(bf16[3,3,128,128]{3,2,1,0:T(8,128)(2,1)} %param.21) | copy-start | bytes 884740
  20.1 0.7 copy-start.7
  20.2 0.7 copy-start.8
  22.1 8.9 %collective-permute-start.2 = (bf16[16,2,256]{2,1,0:T(2,128)(2,1)S(1)}, bf16[16,2,256]{2,1,0:T(2,128)(2,1)S(1)}, u32[]{:S(2)}, u32[]{:S(2)}) collective-permute-start(bf16[16,2,256]{2,1,0:T(2,128)(2,1)S(1)} %get-tuple-element.29), channel_id=1, source_target_pairs={{0,1},{1,2},{2,3},{3,4},{4,5},{5,6},{6,7},{8,9},{9,10},{10,11},{11... | collective-permute-start | bytes 49160 | tf_op jit(solution)/shard_map/ppermute | solution.py:32
  28.9 5.1 %collective-permute-start.3 = (bf16[16,2,256]{2,1,0:T(2,128)(2,1)S(1)}, bf16[16,2,256]{2,1,0:T(2,128)(2,1)S(1)}, u32[]{:S(2)}, u32[]{:S(2)}) collective-permute-start(bf16[16,2,256]{2,1,0:T(2,128)(2,1)S(1)} %get-tuple-element.28), channel_id=1, source_target_pairs={{1,0},{2,1},{3,2},{4,3},{5,4},{6,5},{7,6},{9,8},{10,9},{11,10},{12... | collective-permute-start | bytes 49160 | tf_op jit(solution)/shard_map/ppermute | solution.py:32
  73.5 1.0 %copy-start.2 = (bf16[4,256,128]{2,1,0:T(8,128)(2,1)S(1)}, bf16[4,256,128]{2,1,0:T(8,128)(2,1)}, u32[]{:S(2)}) copy-start(bf16[4,256,128]{2,1,0:T(8,128)(2,1)} %param.15) | copy-start | bytes 786436
  73.5 1.0 %copy-start.3 = (bf16[4,256,128]{2,1,0:T(8,128)(2,1)S(1)}, bf16[4,256,128]{2,1,0:T(8,128)(2,1)}, u32[]{:S(2)}) copy-start(bf16[4,256,128]{2,1,0:T(8,128)(2,1)} %param.14) | copy-start | bytes 786436
